TPU v7x, 128 devices: a whole 4x4x4 slice. The times are simulated.
128 devices in a mesh: cmp: 32 (over y, z, x_lo), tgt: 4 (over x_hi, core).
Axes of the slice: x: 4 (x_hi: 2, x_lo: 2; x = x_hi * 2 + x_lo), y: 4, z: 4, core: 2. Of those that a mesh axis runs over, the one named last changes fastest.
Arguments:
- activity: bfloat16 [8192, 2048], P('cmp', 'tgt'), may hold values from -6 to 6
- drug_basis: bfloat16 [8192, 512], P('cmp'), as said below
- target_basis: bfloat16 [2048, 2048], P('tgt'), as said below
- drug_values: float32 [512], replicated, may hold values from 0.05 to 20
- target_values: float32 [2048], replicated, may hold values from 0.05 to 20
- ridge: float32 [1], replicated, may hold values from 0.5 to 2
Outputs:
- fitted: bfloat16 [8192, 2048], P('cmp', 'tgt')
- loo_residual: bfloat16 [8192, 2048], P('cmp', 'tgt')
Inputs may be any that keep to these rules, and one draw needn't show every extreme that they name: Each row of drug_basis has squared entries summing to at most 0.5. Each row of target_basis has squared entries summing to at most 0.95.
All inputs are finite; a program needn't handle non-finite values.
Results may differ from a plain program's by a relative error of at most 0.002.
Values sent between devices are 32-bit elements; how exact they have to be, the bound alone decides.
No kernel may reach another device: no remote copies, remote signals or barrier semaphores. Data moves between devices by JAX's collectives and lax.ppermute only.
A program may use at most 64 MiB of HBM per device.

v0:
```python
import jax
import jax.numpy as jnp
from jax import lax
from jax.sharding import PartitionSpec as P


def shards(activity, drug_basis, target_basis, drug_values, target_values, ridge):
    highest = lax.Precision.HIGHEST
    drug_devices = lax.axis_size("cmp")
    target_devices = lax.axis_size("tgt")
    basis_rank = drug_basis.shape[1]
    target_total = target_basis.shape[1]
    target_local = target_total // target_devices
    drug_share = basis_rank // drug_devices
    target_wide = target_basis.astype(jnp.float32)
    local_values = lax.dynamic_slice_in_dim(
        target_values, lax.axis_index("tgt") * target_local, target_local
    )
    columns = drug_basis
    drug_block = lax.psum_scatter(
        jnp.dot(columns.T, activity, preferred_element_type=jnp.float32),
        "cmp",
        scatter_dimension=0,
        tiled=True,
    )
    columns = target_wide
    coeff_local = lax.psum_scatter(
        jnp.dot(columns.T, drug_block.T, precision=highest, preferred_element_type=jnp.float32),
        "tgt",
        scatter_dimension=0,
        tiled=True,
    )
    share_values = lax.dynamic_slice_in_dim(
        drug_values, lax.axis_index("cmp") * drug_share, drug_share
    )
    product = local_values[:, None] * share_values[None, :]
    filtered = product / (product + ridge[0]) * coeff_local
    gathered = lax.all_gather(filtered, "tgt", axis=0, tiled=True)
    back_local = jnp.dot(
        target_wide, gathered, precision=highest, preferred_element_type=jnp.float32
    )
    columns = drug_basis
    fitted_full = jnp.dot(
        columns,
        lax.all_gather(back_local, "cmp", axis=1, tiled=True).T,
        precision=highest,
        preferred_element_type=jnp.float32,
    )
    target_squares = target_wide * target_wide
    product = drug_values[:, None] * target_values[None, :]
    spectral_filter = product / (product + ridge[0])
    lever_cols = jnp.dot(
        spectral_filter, target_squares.T, precision=highest, preferred_element_type=jnp.float32
    )
    drug_wide = drug_basis.astype(jnp.float32)
    drug_squares = drug_wide * drug_wide
    leverage = jnp.dot(
        drug_squares, lever_cols, precision=highest, preferred_element_type=jnp.float32
    )
    loo_residual = (activity.astype(jnp.float32) - fitted_full) / (1.0 - leverage)
    return (fitted_full.astype(jnp.bfloat16), loo_residual.astype(jnp.bfloat16))


def solution(mesh):
    return jax.shard_map(
        shards,
        mesh=mesh,
        in_specs=(P("cmp", "tgt"), P("cmp", None), P("tgt", None), P(), P(), P()),
        out_specs=(P("cmp", "tgt"), P("cmp", "tgt")),
        check_vma=False,
    )
```

profile of v0, /device:TPU:0, one launch (start us, length us, event | category | flops | bytes accessed | tf_op | source)
XLA Modules:
  0.0 373.7 jit_solution(9736908890377741233)
XLA Ops:
  7.2 0.0 copy-start
  7.2 0.0 reduce-scatter.3.cloned.1.call-start
  7.2 2.5 fusion.13
  9.7 0.0 copy-start.4
  9.7 0.0 reduce-scatter.3.cloned.1.call-update
  9.7 0.0 copy-start.1
  9.7 0.0 reduce-scatter.5.cloned.1.call-start
  9.8 164.8 %reduce-scatter.3.cloned.1.call-done = f32[16,512]{1,0:T(8,128)} async-done(((f32[512,512]{1,0:T(8,128)}), f32[16,512]{1,0:T(8,128)}) %reduce-scatter.3.cloned.1.call-update) | async-done | bytes 32784 | tf_op jit(solution)/shard_map/reduce_scatter | solution.py:20
  174.6 0.0 copy-done
  174.6 2.3 convolution_bitcast_fusion
  177.0 0.0 reduce-scatter.5.cloned.1.call-update
  177.0 0.0 all-gather.2.cloned.1.call-start
  177.7 0.0 copy-done.4
  177.7 0.1 dynamic_slice.7
  177.8 0.0 copy-done.3
  177.8 0.1 dynamic_slice.6
  177.9 22.7 %reduce-scatter.5.cloned.1.call-done = f32[512,16]{0,1:T(8,128)} async-done(((f32[2048,16]{0,1:T(8,128)}), f32[512,16]{0,1:T(8,128)}) %reduce-scatter.5.cloned.1.call-update) | async-done | bytes 32784 | tf_op jit(solution)/shard_map/reduce_scatter | solution.py:27
  200.5 0.8 fusion.11
  201.4 6.9 %all_gather.6 = f32[2048,16]{0,1:T(8,128)S(1)} all-gather(f32[512,16]{0,1:T(8,128)S(1)} %fusion.11), channel_id=1, replica_groups=mesh['cmp'=32,'tgt'=4] {'tgt'}, dimensions={0}, use_global_device_ids=true | all-gather | bytes 163840 | tf_op jit(solution)/shard_map/all_gather | solution.py:38
  208.3 2.4 convolution_bitcast_fusion.2
  210.6 0.0 all-gather.2.cloned.1.call-update
  210.7 0.0 copy-done.1
  210.7 0.1 copy.12
  210.8 0.0 copy-start.2
  210.8 8.5 %fusion = f32[512,512]{1,0:T(8,128)} fusion(bf16[512,2048]{1,0:T(8,128)(2,1)S(1)} %copy-done, f32[]{:T(128)} %bitcast.17, f32[2048]{0:T(1024)S(1)} %copy-done.3, f32[512]{0:T(512)S(1)} %copy-done.4), kind=kOutput, calls=%fused_computation.1 | convolution fusion | flops 6447693824 | bytes 3155972 | tf_op jit(solution)/shard_map/dot_general | solution.py:52
  219.3 142.1 %all-gather.2.cloned.1.call-done = f32[512,512]{0,1:T(8,128)} async-done(((f32[512,16]{0,1:T(8,128)}), f32[512,512]{0,1:T(8,128)}) %all-gather.2.cloned.1.call-update) | async-done | bytes 1048592 | tf_op jit(solution)/shard_map/all_gather | solution.py:45
  361.5 0.0 copy-done.2
  361.5 2.2 fusion.12
  363.7 0.8 copy.14
  364.5 0.0 copy-done.5
  364.5 1.8 fusion.8
  366.4 0.8 copy.15
  (2 shorter events, 0.0 us)
Async XLA Ops:
  7.2 167.5 %copy-start = (bf16[512,2048]{1,0:T(8,128)(2,1)S(1)}, bf16[512,2048]{1,0:T(8,128)(2,1)}, u32[]{:S(2)}) copy-start(bf16[512,2048]{1,0:T(8,128)(2,1)} %param.8) | copy-start | bytes 6291460
  7.2 167.5 %reduce-scatter.3.cloned.1.call-start = ((), (), s32[]{:S(2)}) async-start(), calls=%async_computation.2 | async-start | bytes 1081344 | tf_op jit(solution)/shard_map/reduce_scatter | solution.py:20
  9.7 168.0 %copy-start.4 = (f32[512]{0:T(512)S(1)}, f32[512]{0:T(512)}, u32[]{:S(2)}) copy-start(f32[512]{0:T(512)} %param.9) | copy-start | bytes 6148
  9.7 168.1 %copy-start.3 = (f32[2048]{0:T(1024)S(1)}, f32[2048]{0:T(1024)}, u32[]{:S(2)}) copy-start(f32[2048]{0:T(1024)} %param.10) | copy-start | bytes 24580
  9.7 200.9 %copy-start.1 = (bf16[256,512]{1,0:T(8,128)(2,1)S(1)}, bf16[256,512]{1,0:T(8,128)(2,1)}, u32[]{:S(2)}) copy-start(bf16[256,512]{1,0:T(8,128)(2,1)} %param.6) | copy-start | bytes 786436
  9.7 190.8 %reduce-scatter.5.cloned.1.call-start = ((), (), s32[]{:S(2)}) async-start(), calls=%async_computation.3 | async-start | bytes 163840 | tf_op jit(solution)/shard_map/reduce_scatter | solution.py:27
  177.0 184.5 %all-gather.2.cloned.1.call-start = ((), (), s32[]{:S(2)}) async-start(), calls=%async_computation.4 | async-start | bytes 1081344 | tf_op jit(solution)/shard_map/all_gather | solution.py:45
  210.8 150.7 %copy-start.2 = (bf16[256,512]{1,0:T(8,128)(2,1)S(1)}, bf16[256,512]{1,0:T(8,128)(2,1)}, u32[]{:S(2)}) copy-start(bf16[256,512]{1,0:T(8,128)(2,1)} %param.7) | copy-start | bytes 786436
  219.3 145.2 %copy-start.5 = (f32[512,512]{1,0:T(8,128)S(1)}, f32[512,512]{1,0:T(8,128)}, u32[]{:S(2)}) copy-start(f32[512,512]{1,0:T(8,128)} %fusion) | copy-start | bytes 3145732
Sparse Core Ops, SparseCore 0:
  10.4 164.2 reduce-scatter.2
  177.9 22.5 reduce-scatter.4
  210.8 150.6 all-gather.1
where the time goes:
time: 374 us
  waiting for transfers between devices  330 us (88%)
  matrix products  19.7 us (5%)
  between operations  14.5 us (4%)
  blocking collectives  6.93 us (2%)
    reduce_scatter x1, waiting for transfers between devices, shards(): lax.psum_scatter(jnp.dot(columns.T, activity, preferred_element_type=jnp....  165 us
    all_gather x1, waiting for transfers between devices, shards(): lax.all_gather(back_local, 'cmp', axis=1, tiled=True)  142 us
    reduce_scatter x1, waiting for transfers between devices, shards(): lax.psum_scatter(jnp.dot(columns.T, drug_block.T, precision=highest, pref...  22.7 us
    dot_general x1, matrix products, shards(): jnp.dot(spectral_filter, target_squares.T, precision=highest, preferred_e...  8.51 us
  transfers between devices with their start and end apart: 3, of which 3 were waited for; matrix products, arithmetic and copies ran while one was open for 2% of the time, Pallas kernels for 0%

commit v1 on v0

v1 whole, which is shorter than its diff:
```python
import jax
import jax.numpy as jnp
from jax import lax
from jax.sharding import PartitionSpec as P


def halves(x):
    high = lax.reduce_precision(x, exponent_bits=8, mantissa_bits=7)
    return high.astype(jnp.bfloat16), (x - high).astype(jnp.bfloat16)


def dot(a, b, dims):
    return lax.dot_general(a, b, (dims, ((), ())), preferred_element_type=jnp.float32)


def shards(activity, drug_basis, target_basis, drug_values, target_values, ridge):
    drug_devices = lax.axis_size("cmp")
    target_devices = lax.axis_size("tgt")
    basis_rank = drug_basis.shape[1]
    target_local = target_basis.shape[0]
    drug_share = basis_rank // drug_devices
    drug_part = dot(drug_basis, activity, ((0,), (0,)))
    drug_parts = lax.all_to_all(
        drug_part.reshape(drug_devices, drug_share, target_local), "cmp", 0, 0
    )
    drug_block = drug_parts.sum(axis=0)
    high, low = halves(drug_block)
    coeff = dot(high, target_basis, ((1,), (0,))) + dot(low, target_basis, ((1,), (0,)))
    coeff = coeff + lax.ppermute(coeff, "tgt", [(i, i ^ 1) for i in range(target_devices)])
    coeff = coeff + lax.ppermute(coeff, "tgt", [(i, i ^ 2) for i in range(target_devices)])
    share_values = lax.dynamic_slice_in_dim(
        drug_values, lax.axis_index("cmp") * drug_share, drug_share
    )
    product = share_values[:, None] * target_values[None, :]
    filtered = product / (product + ridge[0]) * coeff
    high, low = halves(filtered)
    back = dot(high, target_basis, ((1,), (1,))) + dot(low, target_basis, ((1,), (1,)))
    back = lax.all_to_all(
        jnp.broadcast_to(back[None], (drug_devices, drug_share, target_local)), "cmp", 0, 0
    )
    high, low = halves(back.reshape(basis_rank, target_local))
    fitted_full = dot(drug_basis, high, ((1,), (0,))) + dot(drug_basis, low, ((1,), (0,)))
    target_wide = target_basis.astype(jnp.float32)
    square_high, square_low = halves(target_wide * target_wide)
    product = drug_values[:, None] * target_values[None, :]
    filter_high, filter_low = halves(product / (product + ridge[0]))
    lever_cols = (
        dot(filter_high, square_high, ((1,), (1,)))
        + dot(filter_high, square_low, ((1,), (1,)))
        + dot(filter_low, square_high, ((1,), (1,)))
    )
    lever_high, lever_low = halves(lever_cols)
    drug_wide = drug_basis.astype(jnp.float32)
    square_high, square_low = halves(drug_wide * drug_wide)
    leverage = (
        dot(square_high, lever_high, ((1,), (0,)))
        + dot(square_high, lever_low, ((1,), (0,)))
        + dot(square_low, lever_high, ((1,), (0,)))
    )
    loo_residual = (activity.astype(jnp.float32) - fitted_full) / (1.0 - leverage)
    return (fitted_full.astype(jnp.bfloat16), loo_residual.astype(jnp.bfloat16))


def solution(mesh):
    return jax.shard_map(
        shards,
        mesh=mesh,
        in_specs=(P("cmp", "tgt"), P("cmp", None), P("tgt", None), P(), P(), P()),
        out_specs=(P("cmp", "tgt"), P("cmp", "tgt")),
        check_vma=False,
    )
```

time: 374 us -> 71.9 us (0.19)
  waiting for transfers between devices: 330 us -> 33.1 us
  starting transfers between devices: 0.12 us -> 16.8 us
  between operations: 14.5 us -> 1.43 us
  blocking collectives: 6.93 us -> 0 us
  matrix products: 19.7 us -> 14.8 us
    reduce_scatter x2 -> x0, waiting for transfers between devices: 187 us -> none  [the longest x1 165 us: shards(): lax.psum_scatter(jnp.dot(columns.T, activity, preferred_element_type=jnp....]
    all_gather x1 -> x0, waiting for transfers between devices: 142 us -> none  [shards(): lax.all_gather(back_local, 'cmp', axis=1, tiled=True)]
    all_to_all x0 -> x2, waiting for transfers between devices: none -> 31.7 us  [the longest x1 17.2 us: shards(): lax.all_to_all(drug_part.reshape(drug_devices, drug_share, target_local),...]
    all_to_all x0 -> x2, starting transfers between devices: none -> 14 us  [the longest x1 9.34 us: shards(): lax.all_to_all(drug_part.reshape(drug_devices, drug_share, target_local),...]
    all_gather x1 -> x0, blocking collectives: 6.93 us -> none  [shards(): gathered = lax.all_gather(filtered, 'tgt', axis=0, tiled=True)]
    dot_general x6 -> x13, matrix products: 19.7 us -> 14.8 us  [dot(): lax.dot_general(a, b, (dims, ((), ())), preferred_element_type=jnp.float32)]
  transfers between devices with their start and end apart: 3 -> 4, of which waited for: 3 -> 3; matrix products, arithmetic and copies ran while one was open for 2% -> 11% of each run, Pallas kernels for 0% -> 0%
where the time goes in v1:
time: 71.9 us; the launch traced here: 71.4 us
  waiting for transfers between devices  33.1 us (46%)
  starting transfers between devices  16.8 us (23%)
  matrix products  14.8 us (21%)
  local copies, waits for them, and re-layouts  3.8 us (5%)
  other arithmetic  1.46 us (2%)
  between operations  1.43 us (2%)
    all_to_all x1, waiting for transfers between devices, shards(): lax.all_to_all(drug_part.reshape(drug_devices, drug_share, target_local),...  17.2 us
    dot_general x13, matrix products, dot(): lax.dot_general(a, b, (dims, ((), ())), preferred_element_type=jnp.float32)  14.8 us
    all_to_all x1, waiting for transfers between devices, shards(): lax.all_to_all(jnp.broadcast_to(back[None], (drug_devices, drug_share, ta...  14.5 us
    all_to_all x1, starting transfers between devices, shards(): lax.all_to_all(drug_part.reshape(drug_devices, drug_share, target_local),...  9.34 us
    all_to_all x1, starting transfers between devices, shards(): lax.all_to_all(jnp.broadcast_to(back[None], (drug_devices, drug_share, ta...  4.68 us
    ppermute x1, starting transfers between devices, shards(): lax.ppermute(coeff, 'tgt', [(i, i ^ 2) for i in range(target_devices)])  2.81 us
    unnamed x13, local copies, waits for them, and re-layouts  2.56 us
  transfers between devices with their start and end apart: 4, of which 3 were waited for; matrix products, arithmetic and copies ran while one was open for 11% of the time, Pallas kernels for 0%

profile of v1, /device:TPU:0, one launch (start us, length us, event | category | flops | bytes accessed | tf_op | source)
XLA Modules:
  0.0 71.4 jit_solution(16140088185775227378)
XLA Ops:
  0.6 0.0 copy-start
  0.6 2.5 %fusion.34 = f32[512,512]{1,0:T(8,128)} fusion(bf16[256,512]{1,0:T(8,128)(2,1)} %param.7, bf16[256,512]{1,0:T(8,128)(2,1)} %param.6), kind=kOutput, calls=%fused_computation.47 | convolution fusion | flops 134217728 | bytes 1572864 | tf_op jit(solution)/shard_map/dot_general | solution.py:13
  3.1 9.3 %all-to-all-start = ((f32[32,16,512]{2,1,0:T(8,128)}), f32[32,16,512]{2,1,0:T(8,128)S(1)}, u32[]{:S(2)}, u32[]{:S(2)}) async-start(f32[32,16,512]{2,1,0:T(8,128)} %bitcast.22), calls=%async_computation | async-start | bytes 2097152 | tf_op jit(solution)/shard_map/all_to_all | solution.py:23
  13.1 17.2 %all-to-all-done = f32[32,16,512]{2,1,0:T(8,128)S(1)} async-done(((f32[32,16,512]{2,1,0:T(8,128)}), f32[32,16,512]{2,1,0:T(8,128)S(1)}, u32[]{:S(2)}, u32[]{:S(2)}) %all-to-all-start) | async-done | bytes 1048608 | tf_op jit(solution)/shard_map/all_to_all | solution.py:23
  30.3 0.1 reduce_sum.9
  30.4 0.0 copy-start.3
  30.4 0.0 copy-start.4
  30.5 0.4 fusion.30
  30.8 0.4 convolution_add_fusion
  31.2 0.0 collective-permute-start
  31.3 1.5 %fusion.4 = f32[512,512]{1,0:T(8,128)S(1)} fusion(bf16[512,2048]{1,0:T(8,128)(2,1)S(1)} %copy-done, f32[]{:T(128)} %bitcast.20, f32[2048]{0:T(1024)S(1)} %copy-done.3, f32[512]{0:T(512)S(1)} %copy-done.4), kind=kOutput, calls=%fused_computation.10 | convolution fusion | flops 1084227584 | bytes 3155972 | tf_op jit(solution)/shard_map/dot_general | solution.py:13
  32.8 0.0 collective-permute-done
  32.8 2.8 %collective-permute-start.1 = (f32[16,2048]{1,0:T(8,128)S(1)}, f32[16,2048]{1,0:T(8,128)S(1)}, u32[]{:S(2)}, u32[]{:S(2)}) collective-permute-start(f32[16,2048]{1,0:T(8,128)S(1)} %add.49), channel_id=1, source_target_pairs={{0,2},{1,3},{2,0},{3,1},{4,6},{5,7},{6,4},{7,5},{8,10},{9,11},{10,... | collective-permute-start | bytes 393224 | tf_op jit(solution)/shard_map/ppermute | solution.py:30
  35.6 2.3 %fusion.10 = f32[512,512]{1,0:T(8,128)} fusion(f32[512,512]{1,0:T(8,128)S(1)} %fusion.4, bf16[512,2048]{1,0:T(8,128)(2,1)S(1)} %copy-done, f32[]{:T(128)} %bitcast.18, f32[2048]{0:T(1024)S(1)} %copy-done.3, f32[512]{0:T(512)S(1)} %copy-done.4), kind=kOutput, calls=%fused_computation.19 | convolution fusion | flops 1083441152 | bytes 4204548 | tf_op jit(solution)/shard_map/dot_general | solution.py:13
  37.9 0.8 %copy.8 = bf16[256,512]{0,1:T(8,128)(2,1)} copy(bf16[256,512]{1,0:T(8,128)(2,1)S(1)} %copy-done.2) | data formatting | bytes 524288 | tf_op args[0]
  38.8 0.1 dynamic_slice.3
  38.8 1.4 %collective-permute-done.1 = f32[16,2048]{1,0:T(8,128)S(1)} collective-permute-done((f32[16,2048]{1,0:T(8,128)S(1)}, f32[16,2048]{1,0:T(8,128)S(1)}, u32[]{:S(2)}, u32[]{:S(2)}) %collective-permute-start.1) | collective-permute-done | bytes 131104 | tf_op jit(solution)/shard_map/ppermute | solution.py:30
  40.2 0.7 fusion.26
  40.9 0.7 convolution_add_fusion.4
  41.6 1.2 %broadcast_in_dim.2 = f32[32,16,512]{2,1,0:T(8,128)} broadcast(f32[16,512]{1,0:T(8,128)S(1)} %convolution_add_fusion.4), dimensions={1,2} | broadcast | bytes 1081344 | tf_op jit(solution)/shard_map/broadcast_in_dim | solution.py:39
  42.7 4.7 %all-to-all-start.1 = ((f32[32,16,512]{2,1,0:T(8,128)}), f32[32,16,512]{2,1,0:T(8,128)}, u32[]{:S(2)}, u32[]{:S(2)}) async-start(f32[32,16,512]{2,1,0:T(8,128)} %broadcast_in_dim.2), calls=%async_computation.1 | async-start | bytes 2097152 | tf_op jit(solution)/shard_map/all_to_all | solution.py:38
  47.4 0.0 copy-start.1
  47.4 2.7 %fusion.11 = f32[512,512]{1,0:T(8,128)S(1)} fusion(f32[512,512]{1,0:T(8,128)} %fusion.10, bf16[512,2048]{1,0:T(8,128)(2,1)S(1)} %copy-done, f32[]{:T(128)} %bitcast.19, f32[2048]{0:T(1024)S(1)} %copy-done.3, f32[512]{0:T(512)S(1)} %copy-done.4), kind=kOutput, calls=%fused_computation.20 | convolution fusion | flops 1084489728 | bytes 4204548 | tf_op jit(solution)/shard_map/dot_general | solution.py:13
  50.1 0.4 fusion.23
  50.5 0.4 convolution_add_fusion.2
  50.9 14.5 %all-to-all-done.1 = f32[32,16,512]{2,1,0:T(8,128)} async-done(((f32[32,16,512]{2,1,0:T(8,128)}), f32[32,16,512]{2,1,0:T(8,128)}, u32[]{:S(2)}, u32[]{:S(2)}) %all-to-all-start.1) | async-done | bytes 1048608 | tf_op jit(solution)/shard_map/all_to_all | solution.py:38
  65.4 1.4 %fusion.18 = (bf16[512,512]{1,0:T(8,128)(2,1)S(1)}, bf16[512,512]{1,0:T(8,128)(2,1)S(1)}) fusion(f32[32,16,512]{2,1,0:T(8,128)} %all-to-all-done.1), kind=kLoop, calls=%fused_computation.29 | loop fusion | flops 1048576 | bytes 2097152 | tf_op jit(solution)/shard_map/convert_element_type | solution.py:9
  66.8 0.3 fusion.35
  67.1 1.1 %fusion.33 = (bf16[256,512]{0,1:T(8,128)(2,1)S(1)}, f32[256,512]{0,1:T(8,128)}) fusion(f32[512,256]{1,0:T(8,128)S(1)} %fusion.35, bf16[512,512]{1,0:T(8,128)(2,1)S(1)} %get-tuple-element.4, bf16[256,512]{1,0:T(8,128)(2,1)S(1)} %copy-done.1), kind=kOutput, calls=%fused_computation.46 | convolution fusion | flops 134479872 | bytes 2097152 | tf_op jit(solution)/shard_map/dot_general | solution.py:13
  68.3 0.8 %copy.12 = bf16[256,512]{1,0:T(8,128)(2,1)} copy(bf16[256,512]{0,1:T(8,128)(2,1)S(1)} %get-tuple-element.6) | data formatting | bytes 524288
  69.1 1.5 %fusion.17 = bf16[256,512]{0,1:T(8,128)(2,1)S(1)} fusion(f32[256,512]{0,1:T(8,128)S(1)} %convolution_add_fusion.2, f32[256,512]{0,1:T(8,128)} %get-tuple-element.7, bf16[256,512]{0,1:T(8,128)(2,1)} %copy.8, bf16[256,512]{1,0:T(8,128)(2,1)S(1)} %copy-done.1, f32[512,512]{1,0:T(8,128)S(1)} %fusion.11), kind=kOutput, calls=%fused_computation.27 | convolution fusion | flops 136183808 | bytes 2883584 | tf_op jit(solution)/shard_map/dot_general | solution.py:13
  70.6 0.8 %copy.13 = bf16[256,512]{1,0:T(8,128)(2,1)} copy(bf16[256,512]{0,1:T(8,128)(2,1)S(1)} %fusion.17) | data formatting | bytes 524288
  (7 shorter events, 0.0 us)
Async XLA Ops:
  0.6 29.8 %copy-start = (bf16[512,2048]{1,0:T(8,128)(2,1)S(1)}, bf16[512,2048]{1,0:T(8,128)(2,1)}, u32[]{:S(2)}) copy-start(bf16[512,2048]{1,0:T(8,128)(2,1)} %param.8) | copy-start | bytes 6291460
  3.1 27.2 %all-to-all-start = ((f32[32,16,512]{2,1,0:T(8,128)}), f32[32,16,512]{2,1,0:T(8,128)S(1)}, u32[]{:S(2)}, u32[]{:S(2)}) async-start(f32[32,16,512]{2,1,0:T(8,128)} %bitcast.22), calls=%async_computation | async-start | bytes 2097152 | tf_op jit(solution)/shard_map/all_to_all | solution.py:23
  30.4 0.8 %copy-start.3 = (f32[2048]{0:T(1024)S(1)}, f32[2048]{0:T(1024)}, u32[]{:S(2)}) copy-start(f32[2048]{0:T(1024)} %param.10) | copy-start | bytes 24580
  30.4 0.8 %copy-start.4 = (f32[512]{0:T(512)S(1)}, f32[512]{0:T(512)}, u32[]{:S(2)}) copy-start(f32[512]{0:T(512)} %param.9) | copy-start | bytes 6148
  31.2 1.5 %collective-permute-start = (f32[16,2048]{1,0:T(8,128)S(1)}, f32[16,2048]{1,0:T(8,128)S(1)}, u32[]{:S(2)}, u32[]{:S(2)}) collective-permute-start(f32[16,2048]{1,0:T(8,128)S(1)} %convolution_add_fusion), channel_id=1, source_target_pairs={{0,1},{1,0},{2,3},{3,2},{4,5},{5,4},{6,7},{7,6},{8,9},{9,8},{10,11... | collective-permute-start | bytes 393224 | tf_op jit(solution)/shard_map/ppermute | solution.py:29
  32.8 7.4 %collective-permute-start.1 = (f32[16,2048]{1,0:T(8,128)S(1)}, f32[16,2048]{1,0:T(8,128)S(1)}, u32[]{:S(2)}, u32[]{:S(2)}) collective-permute-start(f32[16,2048]{1,0:T(8,128)S(1)} %add.49), channel_id=1, source_target_pairs={{0,2},{1,3},{2,0},{3,1},{4,6},{5,7},{6,4},{7,5},{8,10},{9,11},{10,... | collective-permute-start | bytes 393224 | tf_op jit(solution)/shard_map/ppermute | solution.py:30
  35.6 2.3 %copy-start.2 = (bf16[256,512]{1,0:T(8,128)(2,1)S(1)}, bf16[256,512]{1,0:T(8,128)(2,1)}, u32[]{:S(2)}) copy-start(bf16[256,512]{1,0:T(8,128)(2,1)} %param.6) | copy-start | bytes 786436
  42.7 22.6 %all-to-all-start.1 = ((f32[32,16,512]{2,1,0:T(8,128)}), f32[32,16,512]{2,1,0:T(8,128)}, u32[]{:S(2)}, u32[]{:S(2)}) async-start(f32[32,16,512]{2,1,0:T(8,128)} %broadcast_in_dim.2), calls=%async_computation.1 | async-start | bytes 2097152 | tf_op jit(solution)/shard_map/all_to_all | solution.py:38
  47.4 2.7 %copy-start.1 = (bf16[256,512]{1,0:T(8,128)(2,1)S(1)}, bf16[256,512]{1,0:T(8,128)(2,1)}, u32[]{:S(2)}) copy-start(bf16[256,512]{1,0:T(8,128)(2,1)} %param.7) | copy-start | bytes 786436

commit v2 on v1

v2 whole, which is shorter than its diff:
```python
import jax
import jax.numpy as jnp
from jax import lax
from jax.experimental import pallas as pl
from jax.experimental.pallas import tpu as pltpu
from jax.sharding import PartitionSpec as P

MIB = 1024 * 1024


def halves(x):
    high = x.astype(jnp.bfloat16)
    return high, (x - high.astype(jnp.float32)).astype(jnp.bfloat16)


def dot(a, b, dims):
    return lax.dot_general(a, b, (dims, ((), ())), preferred_element_type=jnp.float32)


def dot_halves(x, b, dims):
    rows = x.shape[0]
    out = dot(jnp.concatenate(halves(x), axis=0), b, dims)
    return out[:rows] + out[rows:]


def crossed():
    return lax.axis_index("tgt") // 2


def project(drug_basis, activity, out):
    devices, share, _ = out.shape
    sums = dot(drug_basis[...], activity[...], ((0,), (0,)))
    flip = crossed()
    for k in range(devices):
        out[jnp.int32(k) ^ flip] = sums[k * share : (k + 1) * share]


def lever(drug_values, target_values, ridge, target_basis, drug_basis, inverse, weights):
    rank, share = drug_values.shape[1], weights.shape[0]
    values, columns, offset = drug_values[...], target_values[...], ridge[0]

    def spectral(first, rows):
        lane = lax.broadcasted_iota(jnp.int32, (rows, rank), 1)
        row = lax.broadcasted_iota(jnp.int32, (rows, rank), 0)
        own = jnp.where(lane == row + first, values, 0.0).sum(axis=1, keepdims=True)
        product = own * columns
        return product / (product + offset)

    weights[...] = spectral((lax.axis_index("cmp") ^ crossed()) * share, share)
    filter_high, filter_low = halves(spectral(0, rank))
    wide = target_basis[...].astype(jnp.float32)
    square_high, square_low = halves(wide * wide)
    along = ((1,), (1,))
    cols = (
        dot(filter_high, square_high, along)
        + dot(filter_high, square_low, along)
        + dot(filter_low, square_high, along)
    )
    cols_high, cols_low = halves(cols)
    wide = drug_basis[...].astype(jnp.float32)
    square_high, square_low = halves(wide * wide)
    along = ((1,), (0,))
    leverage = (
        dot(square_high, cols_high, along)
        + dot(square_high, cols_low, along)
        + dot(square_low, cols_high, along)
    )
    inverse[...] = 1.0 / (1.0 - leverage)


def forward(parts, target_basis, weights, out):
    out[...] = weights[...] * dot_halves(parts[...].sum(axis=0), target_basis[...], ((1,), (0,)))


def backward(mine, other, target_basis, out):
    back = dot_halves(mine[...] + other[...], target_basis[...], ((1,), (1,)))
    out[...] = jnp.broadcast_to(back[None], out.shape)


def fit(parts, drug_basis, activity, inverse, fitted, residual, high, low):
    devices, share, _ = parts.shape
    flip = crossed()
    for k in range(devices):
        rows = pl.ds(k * share, share)
        high[rows], low[rows] = halves(parts[jnp.int32(k) ^ flip])
    basis = drug_basis[...]
    full = dot(basis, high[...], ((1,), (0,))) + dot(basis, low[...], ((1,), (0,)))
    fitted[...] = full.astype(fitted.dtype)
    wide = activity[...].astype(jnp.float32)
    residual[...] = ((wide - full) * inverse[...]).astype(residual.dtype)


def call(body, outs, flops, scratch=(), smem=()):
    def run(*args):
        vmem = pl.BlockSpec(memory_space=pltpu.VMEM)
        scalar = pl.BlockSpec(memory_space=pltpu.SMEM)
        return pl.pallas_call(
            body,
            out_shape=outs,
            in_specs=[scalar if i in smem else vmem for i in range(len(args))],
            out_specs=jax.tree.map(lambda _: vmem, outs),
            scratch_shapes=list(scratch),
            compiler_params=pltpu.CompilerParams(vmem_limit_bytes=40 * MIB),
            cost_estimate=pl.CostEstimate(
                flops=flops, bytes_accessed=sum(x.size * x.dtype.itemsize for x in args), transcendentals=0
            ),
            name=body.__name__,
        )(*args)

    return run


def shards(activity, drug_basis, target_basis, drug_values, target_values, ridge):
    drug_devices = lax.axis_size("cmp")
    target_devices = lax.axis_size("tgt")
    compounds, rank = drug_basis.shape
    targets_here, targets = target_basis.shape
    share = rank // drug_devices
    devices = range(drug_devices * target_devices)
    f32, bf16 = jnp.float32, jnp.bfloat16
    blocks = jax.ShapeDtypeStruct((drug_devices, share, targets_here), f32)
    rows = jax.ShapeDtypeStruct((share, targets), f32)
    here = jax.ShapeDtypeStruct((compounds, targets_here), f32)
    output = jax.ShapeDtypeStruct((compounds, targets_here), bf16)

    sums = call(project, blocks, 2 * compounds * rank * targets_here)(drug_basis, activity)
    parts = lax.all_to_all(sums, "cmp", 0, 0)
    inverse, weights = call(
        lever, (here, rows), 6 * rank * targets_here * (targets + compounds), smem=(2,)
    )(drug_values[None], target_values[None], ridge, target_basis, drug_basis)
    coeff = call(forward, rows, 4 * share * targets_here * targets)(parts, target_basis, weights)
    coeff = coeff + lax.ppermute(coeff, "tgt", [(i, i ^ 1) for i in range(target_devices)])
    across = target_devices | 2
    other = lax.ppermute(coeff, ("cmp", "tgt"), [(i, i ^ across) for i in devices])
    back = call(backward, blocks, 4 * share * targets_here * targets)(coeff, other, target_basis)
    back = lax.all_to_all(back, "cmp", 0, 0)
    scratch = (pltpu.VMEM((rank, targets_here), bf16),) * 2
    return call(fit, (output, output), 4 * compounds * rank * targets_here, scratch)(
        back, drug_basis, activity, inverse
    )


def solution(mesh):
    return jax.shard_map(
        shards,
        mesh=mesh,
        in_specs=(P("cmp", "tgt"), P("cmp", None), P("tgt", None), P(), P(), P()),
        out_specs=(P("cmp", "tgt"), P("cmp", "tgt")),
        check_vma=False,
    )
```

time: 71.9 us -> 62.9 us (0.87)
  blocking collectives: 0 us -> 20.6 us
  waiting for transfers between devices: 33.1 us -> 18.1 us
  matrix products: 14.8 us -> 0 us
  Pallas kernels: 0 us -> 7.14 us
  starting transfers between devices: 16.8 us -> 11.5 us
  other arithmetic: 1.46 us -> 0.02 us
    all_to_all x0 -> x1, blocking collectives: none -> 20.6 us  [shards(): back = lax.all_to_all(back, 'cmp', 0, 0)]
    all_to_all x2 -> x1, waiting for transfers between devices: 31.7 us -> 12.1 us  [shards(): parts = lax.all_to_all(sums, 'cmp', 0, 0)]
    dot_general x13 -> x0, matrix products: 14.8 us -> none  [dot(): lax.dot_general(a, b, (dims, ((), ())), preferred_element_type=jnp.float32)]
    pallas_call x0 -> x5, Pallas kernels: none -> 7.14 us  [run(): pl.pallas_call(body, out_shape=outs, in_specs=[scalar if i in smem else v...]
    all_to_all x2 -> x1, starting transfers between devices: 14 us -> 9.34 us  [shards(): parts = lax.all_to_all(sums, 'cmp', 0, 0)]
    ppermute x1, waiting for transfers between devices: 1.39 us -> 4.73 us  [shards(): lax.ppermute(coeff, ('cmp', 'tgt'), [(i, i ^ across) for i in devices])]
    convert_element_type x1 -> x0, other arithmetic: 1.38 us -> none  [halves(): return (high.astype(jnp.bfloat16), (x - high).astype(jnp.bfloat16))]
    ppermute x1, waiting for transfers between devices: 0.01 us -> 1.36 us  [shards(): lax.ppermute(coeff, 'tgt', [(i, i ^ 1) for i in range(target_devices)])]
  transfers between devices with their start and end apart: 4 -> 3, of which waited for: 3 -> 3; matrix products, arithmetic and copies ran while one was open for 11% -> 0% of each run, Pallas kernels for 0% -> 7%
where the time goes in v2:
time: 62.9 us; the launch traced here: 62.6 us
  blocking collectives  20.6 us (33%)
  waiting for transfers between devices  18.1 us (29%)
  starting transfers between devices  11.5 us (18%)
  Pallas kernels  7.14 us (11%)
  local copies, waits for them, and re-layouts  3.87 us (6%)
  between operations  1.4 us (2%)
    all_to_all x1, blocking collectives, shards(): back = lax.all_to_all(back, 'cmp', 0, 0)  20.6 us
    all_to_all x1, waiting for transfers between devices, shards(): parts = lax.all_to_all(sums, 'cmp', 0, 0)  12.1 us
    all_to_all x1, starting transfers between devices, shards(): parts = lax.all_to_all(sums, 'cmp', 0, 0)  9.34 us
    pallas_call x5, Pallas kernels, run(): pl.pallas_call(body, out_shape=outs, in_specs=[scalar if i in smem else v...  7.14 us
    ppermute x1, waiting for transfers between devices, shards(): lax.ppermute(coeff, ('cmp', 'tgt'), [(i, i ^ across) for i in devices])  4.73 us
    unnamed x20, local copies, waits for them, and re-layouts  3.87 us
    ppermute x1, starting transfers between devices, shards(): lax.ppermute(coeff, ('cmp', 'tgt'), [(i, i ^ across) for i in devices])  2.11 us
    ppermute x1, waiting for transfers between devices, shards(): lax.ppermute(coeff, 'tgt', [(i, i ^ 1) for i in range(target_devices)])  1.36 us
  transfers between devices with their start and end apart: 3, of which 3 were waited for; matrix products, arithmetic and copies ran while one was open for 0% of the time, Pallas kernels for 7%

profile of v2, /device:TPU:0, one launch (start us, length us, event | category | flops | bytes accessed | tf_op | source)
XLA Modules:
  0.0 62.6 jit_solution(14265877687859754235)
XLA Ops:
  0.6 0.0 copy-start
  0.6 0.0 copy-start.2
  0.7 1.1 %copy-done.2 = bf16[256,512]{1,0:T(8,128)(2,1)S(1)} copy-done((bf16[256,512]{1,0:T(8,128)(2,1)S(1)}, bf16[256,512]{1,0:T(8,128)(2,1)}, u32[]{:S(2)}) %copy-start.2) | copy-done | bytes 262168
  1.7 0.0 copy-start.4
  1.7 0.9 %copy-done.4 = bf16[256,512]{1,0:T(8,128)(2,1)S(1)} copy-done((bf16[256,512]{1,0:T(8,128)(2,1)S(1)}, bf16[256,512]{1,0:T(8,128)(2,1)}, u32[]{:S(2)}) %copy-start.4) | copy-done | bytes 262168
  2.7 0.0 copy-start.3
  2.7 0.0 copy-start.8
  2.7 0.0 copy-start.9
  2.7 0.3 project.1
  3.0 0.0 copy-start.1
  3.0 1.0 %copy-done.1 = f32[32,16,512]{2,1,0:T(8,128)} copy-done((f32[32,16,512]{2,1,0:T(8,128)}, f32[32,16,512]{2,1,0:T(8,128)S(1)}, u32[]{:S(2)}) %copy-start.1) | copy-done | bytes 1048600
  4.0 9.3 %all-to-all-start = ((f32[32,16,512]{2,1,0:T(8,128)}), f32[32,16,512]{2,1,0:T(8,128)S(1)}, u32[]{:S(2)}, u32[]{:S(2)}) async-start(f32[32,16,512]{2,1,0:T(8,128)} %copy-done.1), calls=%async_computation | async-start | bytes 2097152 | tf_op jit(solution)/shard_map/all_to_all | solution.py:127
  14.0 0.0 copy-done
  14.0 0.0 copy-done.3
  14.0 0.0 copy-done.8
  14.0 0.0 copy-done.9
  14.0 4.3 %lever.1 = (f32[256,512]{1,0:T(8,128)S(1)}, f32[16,2048]{1,0:T(8,128)S(1)}) custom-call(f32[1,512]{1,0:T(1,128)S(1)} %bitcast.3, f32[1,2048]{1,0:T(1,128)S(1)} %bitcast.2, f32[1]{0:T(128)S(6)} %copy.8.ridge, bf16[512,2048]{1,0:T(8,128)(2,1)S(1)} %copy-done, bf16[256,512]{1,0:T(8,128)(2,1)S(1)} %copy-done.3), custom_call_target="tpu_custom_call" | custom-call | flops 3623878656 | bytes 2369540 | tf_op jit(solution)/shard_map/lever/pallas_call | solution.py:97
  18.3 0.0 copy-start.6
  18.4 0.8 %copy-done.6 = f32[256,512]{1,0:T(8,128)} copy-done((f32[256,512]{1,0:T(8,128)}, f32[256,512]{1,0:T(8,128)S(1)}, u32[]{:S(2)}) %copy-start.6) | copy-done | bytes 524312
  19.2 12.1 %all-to-all-done.parts = f32[32,16,512]{2,1,0:T(8,128)S(1)} async-done(((f32[32,16,512]{2,1,0:T(8,128)}), f32[32,16,512]{2,1,0:T(8,128)S(1)}, u32[]{:S(2)}, u32[]{:S(2)}) %all-to-all-start) | async-done | bytes 1048608 | tf_op jit(solution)/shard_map/all_to_all | solution.py:127
  31.2 0.5 forward.1
  31.7 0.0 collective-permute-start
  31.7 1.4 %collective-permute-done = f32[16,2048]{1,0:T(8,128)S(1)} collective-permute-done((f32[16,2048]{1,0:T(8,128)S(1)}, f32[16,2048]{1,0:T(8,128)S(1)}, u32[]{:S(2)}, u32[]{:S(2)}) %collective-permute-start) | collective-permute-done | bytes 131104 | tf_op jit(solution)/shard_map/ppermute | solution.py:132
  33.1 0.0 copy-start.5
  33.1 0.0 copy-start.7
  33.1 2.1 %collective-permute-start.1 = (f32[16,2048]{1,0:T(8,128)S(1)}, f32[16,2048]{1,0:T(8,128)S(1)}, u32[]{:S(2)}, u32[]{:S(2)}) collective-permute-start(f32[16,2048]{1,0:T(8,128)S(1)} %add.3.mine), channel_id=1, source_target_pairs={{0,6},{1,7},{2,4},{3,5},{4,2},{5,3},{6,0},{7,1},{8,14},{9,15},{10,... | collective-permute-start | bytes 393224 | tf_op jit(solution)/shard_map/ppermute | solution.py:134
  35.2 4.7 %collective-permute-done.1.other = f32[16,2048]{1,0:T(8,128)S(1)} collective-permute-done((f32[16,2048]{1,0:T(8,128)S(1)}, f32[16,2048]{1,0:T(8,128)S(1)}, u32[]{:S(2)}, u32[]{:S(2)}) %collective-permute-start.1) | collective-permute-done | bytes 131104 | tf_op jit(solution)/shard_map/ppermute | solution.py:134
  39.9 0.8 %backward.1 = f32[32,16,512]{2,1,0:T(8,128)S(1)} custom-call(f32[16,2048]{1,0:T(8,128)S(1)} %add.3.mine, f32[16,2048]{1,0:T(8,128)S(1)} %collective-permute-done.1.other, bf16[512,2048]{1,0:T(8,128)(2,1)S(1)} %copy-done), custom_call_target="tpu_custom_call" | custom-call | flops 67108864 | bytes 2359296 | tf_op jit(solution)/shard_map/backward/pallas_call | solution.py:97
  40.8 20.6 %all_to_all.10.parts = f32[32,16,512]{2,1,0:T(8,128)S(1)} all-to-all(f32[32,16,512]{2,1,0:T(8,128)S(1)} %backward.1), channel_id=1, replica_groups=mesh['cmp'=32,'tgt'=4] {'cmp'}, dimensions={0} | all-to-all | bytes 2097152 | tf_op jit(solution)/shard_map/all_to_all | solution.py:136
  61.4 0.0 copy-done.5
  61.4 0.0 copy-done.7
  61.4 1.3 %fit.1 = (bf16[256,512]{1,0:T(8,128)(2,1)}, bf16[256,512]{1,0:T(8,128)(2,1)}) custom-call(f32[32,16,512]{2,1,0:T(8,128)S(1)} %all_to_all.10.parts, bf16[256,512]{1,0:T(8,128)(2,1)S(1)} %copy-done.3, bf16[256,512]{1,0:T(8,128)(2,1)S(1)} %copy-done.5, f32[256,512]{1,0:T(8,128)S(1)} %copy-done.7), custom_call_target="tpu_custom_call" | custom-call | flops 268435456 | bytes 2097152 | tf_op jit(solution)/shard_map/fit/pallas_call | solution.py:97
  (1 shorter events, 0.0 us)
Async XLA Ops:
  0.6 13.4 %copy-start = (bf16[512,2048]{1,0:T(8,128)(2,1)S(1)}, bf16[512,2048]{1,0:T(8,128)(2,1)}, u32[]{:S(2)}) copy-start(bf16[512,2048]{1,0:T(8,128)(2,1)} %target_basis.5) | copy-start | bytes 6291460
  0.6 1.1 %copy-start.2 = (bf16[256,512]{1,0:T(8,128)(2,1)S(1)}, bf16[256,512]{1,0:T(8,128)(2,1)}, u32[]{:S(2)}) copy-start(bf16[256,512]{1,0:T(8,128)(2,1)} %drug_basis.5) | copy-start | bytes 786436
  1.7 0.9 %copy-start.4 = (bf16[256,512]{1,0:T(8,128)(2,1)S(1)}, bf16[256,512]{1,0:T(8,128)(2,1)}, u32[]{:S(2)}) copy-start(bf16[256,512]{1,0:T(8,128)(2,1)} %activity.3) | copy-start | bytes 786436
  2.7 11.3 %copy-start.3 = (bf16[256,512]{1,0:T(8,128)(2,1)S(1)}, bf16[256,512]{1,0:T(8,128)(2,1)}, u32[]{:S(2)}) copy-start(bf16[256,512]{1,0:T(8,128)(2,1)} %drug_basis.5) | copy-start | bytes 786436
  2.7 11.3 %copy-start.8 = (f32[2048]{0:T(1024)S(1)}, f32[2048]{0:T(1024)}, u32[]{:S(2)}) copy-start(f32[2048]{0:T(1024)} %param.10) | copy-start | bytes 24580
  2.7 11.3 %copy-start.9 = (f32[512]{0:T(512)S(1)}, f32[512]{0:T(512)}, u32[]{:S(2)}) copy-start(f32[512]{0:T(512)} %param.9) | copy-start | bytes 6148
  3.0 1.0 %copy-start.1 = (f32[32,16,512]{2,1,0:T(8,128)}, f32[32,16,512]{2,1,0:T(8,128)S(1)}, u32[]{:S(2)}) copy-start(f32[32,16,512]{2,1,0:T(8,128)S(1)} %project.1) | copy-start | bytes 3145732
  4.0 27.2 %all-to-all-start = ((f32[32,16,512]{2,1,0:T(8,128)}), f32[32,16,512]{2,1,0:T(8,128)S(1)}, u32[]{:S(2)}, u32[]{:S(2)}) async-start(f32[32,16,512]{2,1,0:T(8,128)} %copy-done.1), calls=%async_computation | async-start | bytes 2097152 | tf_op jit(solution)/shard_map/all_to_all | solution.py:127
  18.3 0.8 %copy-start.6 = (f32[256,512]{1,0:T(8,128)}, f32[256,512]{1,0:T(8,128)S(1)}, u32[]{:S(2)}) copy-start(f32[256,512]{1,0:T(8,128)S(1)} %get-tuple-element.5.inverse) | copy-start | bytes 1572868
  31.7 1.4 %collective-permute-start = (f32[16,2048]{1,0:T(8,128)S(1)}, f32[16,2048]{1,0:T(8,128)S(1)}, u32[]{:S(2)}, u32[]{:S(2)}) collective-permute-start(f32[16,2048]{1,0:T(8,128)S(1)} %forward.1), channel_id=1, source_target_pairs={{0,1},{1,0},{2,3},{3,2},{4,5},{5,4},{6,7},{7,6},{8,9},{9,8},{10,11... | collective-permute-start | bytes 393224 | tf_op jit(solution)/shard_map/ppermute | solution.py:132
  33.1 28.3 %copy-start.5 = (bf16[256,512]{1,0:T(8,128)(2,1)S(1)}, bf16[256,512]{1,0:T(8,128)(2,1)}, u32[]{:S(2)}) copy-start(bf16[256,512]{1,0:T(8,128)(2,1)} %activity.3) | copy-start | bytes 786436
  33.1 28.3 %copy-start.7 = (f32[256,512]{1,0:T(8,128)S(1)}, f32[256,512]{1,0:T(8,128)}, u32[]{:S(2)}) copy-start(f32[256,512]{1,0:T(8,128)} %copy-done.6) | copy-start | bytes 1572868
  33.1 6.8 %collective-permute-start.1 = (f32[16,2048]{1,0:T(8,128)S(1)}, f32[16,2048]{1,0:T(8,128)S(1)}, u32[]{:S(2)}, u32[]{:S(2)}) collective-permute-start(f32[16,2048]{1,0:T(8,128)S(1)} %add.3.mine), channel_id=1, source_target_pairs={{0,6},{1,7},{2,4},{3,5},{4,2},{5,3},{6,0},{7,1},{8,14},{9,15},{10,... | collective-permute-start | bytes 393224 | tf_op jit(solution)/shard_map/ppermute | solution.py:134

commit v3 on v2

--- a/solution.py
+++ b/solution.py
@@ -27,15 +27,23 @@
     return lax.axis_index("tgt") // 2
 
 
-def project(drug_basis, activity, out):
+def project(drug_basis, activity, out, basis, values, sems):
     devices, share, _ = out.shape
-    sums = dot(drug_basis[...], activity[...], ((0,), (0,)))
+    copies = [
+        pltpu.make_async_copy(drug_basis, basis, sems.at[0]),
+        pltpu.make_async_copy(activity, values, sems.at[1]),
+    ]
+    for copy in copies:
+        copy.start()
+    for copy in copies:
+        copy.wait()
+    sums = dot(basis[...], values[...], ((0,), (0,)))
     flip = crossed()
     for k in range(devices):
         out[jnp.int32(k) ^ flip] = sums[k * share : (k + 1) * share]
 
 
-def lever(drug_values, target_values, ridge, target_basis, drug_basis, inverse, weights):
+def lever(drug_values, target_values, ridge, target_basis, drug_basis, _, inverse, weights):
     rank, share = drug_values.shape[1], weights.shape[0]
     values, columns, offset = drug_values[...], target_values[...], ridge[0]
 
@@ -68,12 +76,12 @@
     inverse[...] = 1.0 / (1.0 - leverage)
 
 
-def forward(parts, target_basis, weights, out):
-    out[...] = weights[...] * dot_halves(parts[...].sum(axis=0), target_basis[...], ((1,), (0,)))
+def forward(parts, target_basis, out):
+    out[...] = dot_halves(parts[...].sum(axis=0), target_basis[...], ((1,), (0,)))
 
 
-def backward(mine, other, target_basis, out):
-    back = dot_halves(mine[...] + other[...], target_basis[...], ((1,), (1,)))
+def backward(mine, other, weights, target_basis, out):
+    back = dot_halves(weights[...] * (mine[...] + other[...]), target_basis[...], ((1,), (1,)))
     out[...] = jnp.broadcast_to(back[None], out.shape)
 
 
@@ -90,15 +98,16 @@
     residual[...] = ((wide - full) * inverse[...]).astype(residual.dtype)
 
 
-def call(body, outs, flops, scratch=(), smem=()):
+def call(body, outs, flops, scratch=(), smem=(), hbm=(), hbm_out=False):
     def run(*args):
         vmem = pl.BlockSpec(memory_space=pltpu.VMEM)
         scalar = pl.BlockSpec(memory_space=pltpu.SMEM)
+        far = pl.BlockSpec(memory_space=pltpu.HBM)
         return pl.pallas_call(
             body,
             out_shape=outs,
-            in_specs=[scalar if i in smem else vmem for i in range(len(args))],
-            out_specs=jax.tree.map(lambda _: vmem, outs),
+            in_specs=[scalar if i in smem else far if i in hbm else vmem for i in range(len(args))],
+            out_specs=jax.tree.map(lambda _: far if hbm_out else vmem, outs),
             scratch_shapes=list(scratch),
             compiler_params=pltpu.CompilerParams(vmem_limit_bytes=40 * MIB),
             cost_estimate=pl.CostEstimate(
@@ -123,16 +132,22 @@
     here = jax.ShapeDtypeStruct((compounds, targets_here), f32)
     output = jax.ShapeDtypeStruct((compounds, targets_here), bf16)
 
-    sums = call(project, blocks, 2 * compounds * rank * targets_here)(drug_basis, activity)
+    scratch = (
+        pltpu.VMEM(drug_basis.shape, bf16),
+        pltpu.VMEM(activity.shape, bf16),
+        pltpu.SemaphoreType.DMA((2,)),
+    )
+    far = [pltpu.with_memory_space_constraint(x, pltpu.HBM) for x in (drug_basis, activity)]
+    sums = call(project, blocks, 2 * compounds * rank * targets_here, scratch, hbm=(0, 1))(*far)
     parts = lax.all_to_all(sums, "cmp", 0, 0)
-    inverse, weights = call(
-        lever, (here, rows), 6 * rank * targets_here * (targets + compounds), smem=(2,)
-    )(drug_values[None], target_values[None], ridge, target_basis, drug_basis)
-    coeff = call(forward, rows, 4 * share * targets_here * targets)(parts, target_basis, weights)
+    coeff = call(forward, rows, 4 * share * targets_here * targets)(parts, target_basis)
     coeff = coeff + lax.ppermute(coeff, "tgt", [(i, i ^ 1) for i in range(target_devices)])
     across = target_devices | 2
+    inverse, weights = call(
+        lever, (here, rows), 6 * rank * targets_here * (targets + compounds), smem=(2,), hbm=(5,)
+    )(drug_values[None], target_values[None], ridge, target_basis, drug_basis, coeff)
     other = lax.ppermute(coeff, ("cmp", "tgt"), [(i, i ^ across) for i in devices])
-    back = call(backward, blocks, 4 * share * targets_here * targets)(coeff, other, target_basis)
+    back = call(backward, blocks, 4 * share * targets_here * targets)(coeff, other, weights, target_basis)
     back = lax.all_to_all(back, "cmp", 0, 0)
     scratch = (pltpu.VMEM((rank, targets_here), bf16),) * 2
     return call(fit, (output, output), 4 * compounds * rank * targets_here, scratch)(

time: 62.9 us -> 61.2 us (0.973)
  blocking collectives: 20.6 us -> 48 us
  waiting for transfers between devices: 18.1 us -> 1.1 us
  starting transfers between devices: 11.5 us -> 2.11 us
  local copies, waits for them, and re-layouts: 3.87 us -> 0.02 us
  Pallas kernels: 7.14 us -> 8.37 us
    all_to_all x0 -> x1, blocking collectives: none -> 27 us  [shards(): parts = lax.all_to_all(sums, 'cmp', 0, 0)]
    all_to_all x1 -> x0, waiting for transfers between devices: 12.1 us -> none  [shards(): parts = lax.all_to_all(sums, 'cmp', 0, 0)]
    all_to_all x1 -> x0, starting transfers between devices: 9.34 us -> none  [shards(): parts = lax.all_to_all(sums, 'cmp', 0, 0)]
    ppermute x1, waiting for transfers between devices: 4.73 us -> 0.4 us  [shards(): lax.ppermute(coeff, ('cmp', 'tgt'), [(i, i ^ across) for i in devices])]
    unnamed x20 -> x10, local copies, waits for them, and re-layouts: 3.87 us -> 0.02 us
    pallas_call x5, Pallas kernels: 7.14 us -> 8.37 us  [run(): pl.pallas_call(body, out_shape=outs, in_specs=[scalar if i in smem else f...]
    ppermute x1, waiting for transfers between devices: 1.36 us -> 0.69 us  [shards(): lax.ppermute(coeff, 'tgt', [(i, i ^ 1) for i in range(target_devices)])]
  transfers between devices with their start and end apart: 3 -> 2, of which waited for: 3 -> 2; matrix products, arithmetic and copies ran while one was open for 0% -> 0% of each run, Pallas kernels for 7% -> 7%
where the time goes in v3:
time: 61.2 us; the launch traced here: 60.9 us
  blocking collectives  48 us (78%)
  Pallas kernels  8.37 us (14%)
  starting transfers between devices  2.11 us (3%)
  between operations  1.35 us (2%)
  waiting for transfers between devices  1.1 us (2%)
    all_to_all x1, blocking collectives, shards(): parts = lax.all_to_all(sums, 'cmp', 0, 0)  27 us
    all_to_all x1, blocking collectives, shards(): back = lax.all_to_all(back, 'cmp', 0, 0)  21 us
    pallas_call x5, Pallas kernels, run(): pl.pallas_call(body, out_shape=outs, in_specs=[scalar if i in smem else f...  8.37 us
    ppermute x1, starting transfers between devices, shards(): lax.ppermute(coeff, ('cmp', 'tgt'), [(i, i ^ across) for i in devices])  2.11 us
  transfers between devices with their start and end apart: 2, of which 2 were waited for; matrix products, arithmetic and copies ran while one was open for 0% of the time, Pallas kernels for 7%

profile of v3, /device:TPU:0, one launch (start us, length us, event | category | flops | bytes accessed | tf_op | source)
XLA Modules:
  0.0 60.9 jit_solution(4616018562993379494)
XLA Ops:
  0.6 0.0 copy-start
  0.6 1.5 %project.1 = f32[32,16,512]{2,1,0:T(8,128)S(1)} custom-call(bf16[256,512]{1,0:T(8,128)(2,1)} %drug_basis.5, bf16[256,512]{1,0:T(8,128)(2,1)} %activity.3), custom_call_target="tpu_custom_call" | custom-call | flops 134217728 | bytes 524288 | tf_op jit(solution)/shard_map/project/pallas_call | solution.py:106
  2.2 27.0 %all_to_all.10.parts = f32[32,16,512]{2,1,0:T(8,128)S(1)} all-to-all(f32[32,16,512]{2,1,0:T(8,128)S(1)} %project.1), channel_id=1, replica_groups=mesh['cmp'=32,'tgt'=4] {'cmp'}, dimensions={0} | all-to-all | bytes 2097152 | tf_op jit(solution)/shard_map/all_to_all | solution.py:142
  29.2 0.0 copy-done
  29.2 0.0 copy-start.1
  29.2 0.0 copy-start.3
  29.2 0.0 copy-start.4
  29.2 0.5 forward.1
  29.7 0.0 collective-permute-start
  30.3 0.7 %collective-permute-done = f32[16,2048]{1,0:T(8,128)S(1)} collective-permute-done((f32[16,2048]{1,0:T(8,128)S(1)}, f32[16,2048]{1,0:T(8,128)S(1)}, u32[]{:S(2)}, u32[]{:S(2)}) %collective-permute-start) | collective-permute-done | bytes 131104 | tf_op jit(solution)/shard_map/ppermute | solution.py:144
  31.1 2.1 %collective-permute-start.1 = (f32[16,2048]{1,0:T(8,128)S(1)}, f32[16,2048]{1,0:T(8,128)S(1)}, u32[]{:S(2)}, u32[]{:S(2)}) collective-permute-start(f32[16,2048]{1,0:T(8,128)S(1)} %add.3._.mine), channel_id=1, source_target_pairs={{0,6},{1,7},{2,4},{3,5},{4,2},{5,3},{6,0},{7,1},{8,14},{9,15},{10,... | collective-permute-start | bytes 393224 | tf_op jit(solution)/shard_map/ppermute | solution.py:149
  33.2 0.0 copy-done.1
  33.2 0.0 copy-done.3
  33.2 0.0 copy-done.4
  33.2 4.3 %lever.1 = (f32[256,512]{1,0:T(8,128)S(1)}, f32[16,2048]{1,0:T(8,128)S(1)}) custom-call(f32[1,512]{1,0:T(1,128)S(1)} %bitcast.3, f32[1,2048]{1,0:T(1,128)S(1)} %bitcast.2, f32[1]{0:T(128)S(6)} %copy.8.ridge, bf16[512,2048]{1,0:T(8,128)(2,1)S(1)} %copy-done, bf16[256,512]{1,0:T(8,128)(2,1)S(1)} %copy-done.1, f32[16,2048]{1,0:T(8,128)S(1)} %add.3._.mine), custom_call_target="tpu_custom_call" | custom-call | flops 3623878656 | bytes 2500612 | tf_op jit(solution)/shard_map/lever/pallas_call | solution.py:106
  37.5 0.4 collective-permute-done.1.other
  37.9 0.0 copy-start.2
  37.9 0.8 %backward.1 = f32[32,16,512]{2,1,0:T(8,128)S(1)} custom-call(f32[16,2048]{1,0:T(8,128)S(1)} %add.3._.mine, f32[16,2048]{1,0:T(8,128)S(1)} %collective-permute-done.1.other, f32[16,2048]{1,0:T(8,128)S(1)} %get-tuple-element.4.weights, bf16[512,2048]{1,0:T(8,128)(2,1)S(1)} %copy-done), custom_call_target="tpu_custom_call" | custom-call | flops 67108864 | bytes 2490368 | tf_op jit(solution)/shard_map/backward/pallas_call | solution.py:106
  38.7 21.0 %all_to_all.11.parts = f32[32,16,512]{2,1,0:T(8,128)S(1)} all-to-all(f32[32,16,512]{2,1,0:T(8,128)S(1)} %backward.1), channel_id=1, replica_groups=mesh['cmp'=32,'tgt'=4] {'cmp'}, dimensions={0} | all-to-all | bytes 2097152 | tf_op jit(solution)/shard_map/all_to_all | solution.py:151
  59.7 0.0 copy-done.2
  59.7 1.3 %fit.1 = (bf16[256,512]{1,0:T(8,128)(2,1)}, bf16[256,512]{1,0:T(8,128)(2,1)}) custom-call(f32[32,16,512]{2,1,0:T(8,128)S(1)} %all_to_all.11.parts, bf16[256,512]{1,0:T(8,128)(2,1)S(1)} %copy-done.1, bf16[256,512]{1,0:T(8,128)(2,1)S(1)} %copy-done.2, f32[256,512]{1,0:T(8,128)S(1)} %get-tuple-element.5.inverse), custom_call_target="tpu_custom_call" | custom-call | flops 268435456 | bytes 2097152 | tf_op jit(solution)/shard_map/fit/pallas_call | solution.py:106
  (1 shorter events, 0.0 us)
Async XLA Ops:
  0.6 28.6 %copy-start = (bf16[512,2048]{1,0:T(8,128)(2,1)S(1)}, bf16[512,2048]{1,0:T(8,128)(2,1)}, u32[]{:S(2)}) copy-start(bf16[512,2048]{1,0:T(8,128)(2,1)} %target_basis.5) | copy-start | bytes 6291460
  29.2 4.0 %copy-start.1 = (bf16[256,512]{1,0:T(8,128)(2,1)S(1)}, bf16[256,512]{1,0:T(8,128)(2,1)}, u32[]{:S(2)}) copy-start(bf16[256,512]{1,0:T(8,128)(2,1)} %drug_basis.5) | copy-start | bytes 786436
  29.2 4.0 %copy-start.3 = (f32[2048]{0:T(1024)S(1)}, f32[2048]{0:T(1024)}, u32[]{:S(2)}) copy-start(f32[2048]{0:T(1024)} %param.10) | copy-start | bytes 24580
  29.2 4.0 %copy-start.4 = (f32[512]{0:T(512)S(1)}, f32[512]{0:T(512)}, u32[]{:S(2)}) copy-start(f32[512]{0:T(512)} %param.9) | copy-start | bytes 6148
  29.7 1.4 %collective-permute-start = (f32[16,2048]{1,0:T(8,128)S(1)}, f32[16,2048]{1,0:T(8,128)S(1)}, u32[]{:S(2)}, u32[]{:S(2)}) collective-permute-start(f32[16,2048]{1,0:T(8,128)S(1)} %forward.1), channel_id=1, source_target_pairs={{0,1},{1,0},{2,3},{3,2},{4,5},{5,4},{6,7},{7,6},{8,9},{9,8},{10,11... | collective-permute-start | bytes 393224 | tf_op jit(solution)/shard_map/ppermute | solution.py:144
  31.1 6.8 %collective-permute-start.1 = (f32[16,2048]{1,0:T(8,128)S(1)}, f32[16,2048]{1,0:T(8,128)S(1)}, u32[]{:S(2)}, u32[]{:S(2)}) collective-permute-start(f32[16,2048]{1,0:T(8,128)S(1)} %add.3._.mine), channel_id=1, source_target_pairs={{0,6},{1,7},{2,4},{3,5},{4,2},{5,3},{6,0},{7,1},{8,14},{9,15},{10,... | collective-permute-start | bytes 393224 | tf_op jit(solution)/shard_map/ppermute | solution.py:149
  37.9 21.8 %copy-start.2 = (bf16[256,512]{1,0:T(8,128)(2,1)S(1)}, bf16[256,512]{1,0:T(8,128)(2,1)}, u32[]{:S(2)}) copy-start(bf16[256,512]{1,0:T(8,128)(2,1)} %activity.3) | copy-start | bytes 786436

commit v4 on v3

v4 whole, which is shorter than its diff:
```python
import jax
import jax.numpy as jnp
from jax import lax
from jax.experimental import pallas as pl
from jax.experimental.pallas import tpu as pltpu
from jax.sharding import PartitionSpec as P

MIB = 1024 * 1024
PIECES = 2


def halves(x):
    high = x.astype(jnp.bfloat16)
    return high, (x - high.astype(jnp.float32)).astype(jnp.bfloat16)


def dot(a, b, along=(1, 0)):
    dims = (((along[0],), (along[1],)), ((), ()))
    return lax.dot_general(a, b, dims, preferred_element_type=jnp.float32)


def dot_halves(x, b):
    rows = x.shape[0]
    out = dot(jnp.concatenate(halves(x), axis=0), b)
    return out[:rows] + out[rows:]


def dot_pairs(a, b):
    rows = a[0].shape[0]
    out = dot(jnp.concatenate(a, axis=0), b[0])
    return out[:rows] + out[rows:] + dot(a[0], b[1])


def core():
    return lax.rem(lax.axis_index("tgt"), 2)


def crossed():
    return lax.axis_index("tgt") // 2


def eigen(drug_values, first, rows):
    rank = drug_values.shape[1]
    lane = lax.broadcasted_iota(jnp.int32, (rows, rank), 1)
    row = lax.broadcasted_iota(jnp.int32, (rows, rank), 0)
    return jnp.where(lane == row + first, drug_values[...], 0.0).sum(axis=1, keepdims=True)


def project(drug_basis, activity, out, basis, values, sems):
    devices, share, _ = out.shape
    copies = [
        pltpu.make_async_copy(drug_basis, basis, sems.at[0]),
        pltpu.make_async_copy(activity, values, sems.at[1]),
    ]
    for copy in copies:
        copy.start()
    for copy in copies:
        copy.wait()
    sums = dot(basis[...], values[...], (0, 0))
    flip = crossed()
    for k in range(devices):
        out[jnp.int32(k) ^ flip] = sums[k * share : (k + 1) * share]


def forward(parts, target_basis, out, turned):
    out[...] = dot_halves(parts[...].sum(axis=0), target_basis[...])

    @pl.when(core() == 1)
    def _():
        turned[...] = target_basis[...].T


def middle(mine, other, target_basis, out, turned):
    out[...] = mine[...] + other[...]

    @pl.when(core() == 0)
    def _():
        turned[...] = target_basis[...].T


def of_core(work, turned_0, turned_1):
    @pl.when(core() == 0)
    def _():
        work(turned_0)

    @pl.when(core() == 1)
    def _():
        work(turned_1)


def lever(drug_values, target_values, ridge, drug_basis, turned_0, turned_1, inverse, weights):
    rank, targets, share = drug_values.shape[1], target_values.shape[1], weights.shape[0]
    offset = ridge[0]
    first = (lax.axis_index("cmp") ^ crossed()) * share
    product = eigen(drug_values, first, share) * target_values[...]
    weights[...] = product / (product + offset)
    wide = drug_basis[...].astype(jnp.float32)
    squares = halves(wide * wide)
    own = eigen(drug_values, 0, rank)

    def work(turned):
        step = targets // PIECES
        total = None
        for start in range(0, targets, step):
            some = slice(start, start + step)
            product = own * target_values[:, some]
            mixed = dot_pairs(squares, halves(product / (product + offset)))
            wide = turned[some].astype(jnp.float32)
            term = dot_pairs(halves(mixed), halves(wide * wide))
            total = term if total is None else total + term
        inverse[...] = 1.0 / (1.0 - total)

    of_core(work, turned_0, turned_1)


def backward(mine, other, weights, turned_0, turned_1, out):
    filtered = weights[...] * (mine[...] + other[...])

    def work(turned):
        out[...] = jnp.broadcast_to(dot_halves(filtered, turned[...])[None], out.shape)

    of_core(work, turned_0, turned_1)


def fit(parts, drug_basis, activity, inverse, fitted, residual, high, low):
    devices, share, _ = parts.shape
    flip = crossed()
    for k in range(devices):
        rows = pl.ds(k * share, share)
        high[rows], low[rows] = halves(parts[jnp.int32(k) ^ flip])
    basis = drug_basis[...]
    full = dot(basis, high[...]) + dot(basis, low[...])
    fitted[...] = full.astype(fitted.dtype)
    wide = activity[...].astype(jnp.float32)
    residual[...] = ((wide - full) * inverse[...]).astype(residual.dtype)


def call(body, outs, flops, scratch=(), far=(), scalar=()):
    def run(*args):
        vmem = pl.BlockSpec(memory_space=pltpu.VMEM)
        spaces = {**dict.fromkeys(far, pl.ANY), **dict.fromkeys(scalar, pltpu.SMEM)}
        return pl.pallas_call(
            body,
            out_shape=outs,
            in_specs=[pl.BlockSpec(memory_space=spaces.get(i, pltpu.VMEM)) for i in range(len(args))],
            out_specs=jax.tree.map(lambda _: vmem, outs),
            scratch_shapes=list(scratch),
            compiler_params=pltpu.CompilerParams(vmem_limit_bytes=40 * MIB),
            cost_estimate=pl.CostEstimate(
                flops=flops, bytes_accessed=sum(x.size * x.dtype.itemsize for x in args), transcendentals=0
            ),
            name=body.__name__,
        )(*args)

    return run


def shards(activity, drug_basis, target_basis, drug_values, target_values, ridge):
    drug_devices = lax.axis_size("cmp")
    target_devices = lax.axis_size("tgt")
    compounds, rank = drug_basis.shape
    targets_here, targets = target_basis.shape
    share = rank // drug_devices
    devices = range(drug_devices * target_devices)
    f32, bf16 = jnp.float32, jnp.bfloat16
    blocks = jax.ShapeDtypeStruct((drug_devices, share, targets_here), f32)
    rows = jax.ShapeDtypeStruct((share, targets), f32)
    here = jax.ShapeDtypeStruct((compounds, targets_here), f32)
    turned = jax.ShapeDtypeStruct((targets, targets_here), bf16)
    output = jax.ShapeDtypeStruct((compounds, targets_here), bf16)

    scratch = (
        pltpu.VMEM(drug_basis.shape, bf16),
        pltpu.VMEM(activity.shape, bf16),
        pltpu.SemaphoreType.DMA((2,)),
    )
    far = [pltpu.with_memory_space_constraint(x, pltpu.HBM) for x in (drug_basis, activity)]
    sums = call(project, blocks, 2 * compounds * rank * targets_here, scratch, far=(0, 1))(*far)
    parts = lax.all_to_all(sums, "cmp", 0, 0)
    flops = 4 * share * targets_here * targets
    coeff, turned_1 = call(forward, (rows, turned), flops)(parts, target_basis)
    other = lax.ppermute(coeff, "tgt", [(i, i ^ 1) for i in range(target_devices)])
    coeff, turned_0 = call(middle, (rows, turned), targets_here * targets)(coeff, other, target_basis)
    across = target_devices | 2
    other = lax.ppermute(coeff, ("cmp", "tgt"), [(i, i ^ across) for i in devices])
    inverse, weights = call(lever, (here, rows), 6 * compounds * rank * targets, scalar=(2,))(
        drug_values[None], target_values[None], ridge, drug_basis, turned_0, turned_1
    )
    back = call(backward, blocks, flops)(coeff, other, weights, turned_0, turned_1)
    back = lax.all_to_all(back, "cmp", 0, 0)
    scratch = (pltpu.VMEM((rank, targets_here), bf16),) * 2
    return call(fit, (output, output), 4 * compounds * rank * targets_here, scratch)(
        back, drug_basis, activity, inverse
    )


def solution(mesh):
    return jax.shard_map(
        shards,
        mesh=mesh,
        in_specs=(P("cmp", "tgt"), P("cmp", None), P("tgt", None), P(), P(), P()),
        out_specs=(P("cmp", "tgt"), P("cmp", "tgt")),
        check_vma=False,
    )
```

time: 61.2 us -> 60.5 us (0.989)
    pallas_call x5 -> x6, Pallas kernels: 8.37 us -> 8.2 us  [run(): pl.pallas_call(body, out_shape=outs, in_specs=[pl.BlockSpec(memory_space=...]
  transfers between devices with their start and end apart: 2 -> 2, of which waited for: 2 -> 2; matrix products, arithmetic and copies ran while one was open for 0% -> 0% of each run, Pallas kernels for 7% -> 6%
where the time goes in v4:
time: 60.5 us; the launch traced here: 60.3 us
  blocking collectives  47.5 us (79%)
  Pallas kernels  8.2 us (14%)
  starting transfers between devices  2.11 us (3%)
  between operations  1.36 us (2%)
  waiting for transfers between devices  1.04 us (2%)
    all_to_all x1, blocking collectives, shards(): parts = lax.all_to_all(sums, 'cmp', 0, 0)  27 us
    all_to_all x1, blocking collectives, shards(): back = lax.all_to_all(back, 'cmp', 0, 0)  20.5 us
    pallas_call x6, Pallas kernels, run(): pl.pallas_call(body, out_shape=outs, in_specs=[pl.BlockSpec(memory_space=...  8.2 us
    ppermute x1, starting transfers between devices, shards(): lax.ppermute(coeff, ('cmp', 'tgt'), [(i, i ^ across) for i in devices])  2.11 us
  transfers between devices with their start and end apart: 2, of which 2 were waited for; matrix products, arithmetic and copies ran while one was open for 0% of the time, Pallas kernels for 6%

profile of v4, /device:TPU:0, one launch (start us, length us, event | category | flops | bytes accessed | tf_op | source)
XLA Modules:
  0.0 60.3 jit_solution(16814821088920492923)
XLA Ops:
  0.6 0.0 copy-start
  0.6 1.5 %project.1 = f32[32,16,512]{2,1,0:T(8,128)S(1)} custom-call(bf16[256,512]{1,0:T(8,128)(2,1)} %drug_basis.5, bf16[256,512]{1,0:T(8,128)(2,1)} %activity.3), custom_call_target="tpu_custom_call" | custom-call | flops 134217728 | bytes 524288 | tf_op jit(solution)/shard_map/project/pallas_call | solution.py:142
  2.2 27.0 %all_to_all.10.parts = f32[32,16,512]{2,1,0:T(8,128)S(1)} all-to-all(f32[32,16,512]{2,1,0:T(8,128)S(1)} %project.1), channel_id=1, replica_groups=mesh['cmp'=32,'tgt'=4] {'cmp'}, dimensions={0} | all-to-all | bytes 2097152 | tf_op jit(solution)/shard_map/all_to_all | solution.py:179
  29.2 0.0 copy-done
  29.2 0.0 copy-start.1
  29.2 0.0 copy-start.3
  29.2 0.0 copy-start.4
  29.2 0.5 forward.1
  29.7 0.0 collective-permute-start
  30.3 0.7 %collective-permute-done.other = f32[16,2048]{1,0:T(8,128)S(1)} collective-permute-done((f32[16,2048]{1,0:T(8,128)S(1)}, f32[16,2048]{1,0:T(8,128)S(1)}, u32[]{:S(2)}, u32[]{:S(2)}) %collective-permute-start) | collective-permute-done | bytes 131104 | tf_op jit(solution)/shard_map/ppermute | solution.py:182
  31.0 0.6 %middle.1 = (f32[16,2048]{1,0:T(8,128)S(1)}, bf16[2048,512]{1,0:T(8,128)(2,1)S(1)}) custom-call(f32[16,2048]{1,0:T(8,128)S(1)} %get-tuple-element.8.mine, f32[16,2048]{1,0:T(8,128)S(1)} %collective-permute-done.other, bf16[512,2048]{1,0:T(8,128)(2,1)S(1)} %copy-done), custom_call_target="tpu_custom_call" | custom-call | flops 1048576 | bytes 2359296 | tf_op jit(solution)/shard_map/middle/pallas_call | solution.py:142
  31.6 2.1 %collective-permute-start.1 = (f32[16,2048]{1,0:T(8,128)S(1)}, f32[16,2048]{1,0:T(8,128)S(1)}, u32[]{:S(2)}, u32[]{:S(2)}) collective-permute-start(f32[16,2048]{1,0:T(8,128)S(1)} %get-tuple-element.9.mine), channel_id=1, source_target_pairs={{0,6},{1,7},{2,4},{3,5},{4,2},{5,3},{6,0},{7,1},{8,14},{9,15},{10,... | collective-permute-start | bytes 393224 | tf_op jit(solution)/shard_map/ppermute | solution.py:185
  33.8 0.0 copy-done.1
  33.8 0.0 copy-done.3
  33.8 0.0 copy-done.4
  33.8 3.8 %lever.1 = (f32[256,512]{1,0:T(8,128)S(1)}, f32[16,2048]{1,0:T(8,128)S(1)}) custom-call(f32[1,512]{1,0:T(1,128)S(1)} %bitcast.3, f32[1,2048]{1,0:T(1,128)S(1)} %bitcast.2, f32[1]{0:T(128)S(6)} %copy.8.ridge, bf16[256,512]{1,0:T(8,128)(2,1)S(1)} %copy-done.1, bf16[2048,512]{1,0:T(8,128)(2,1)S(1)} %get-tuple-element.10.turned_0, ...), custom_call_target="tpu_custom_call" | custom-call | flops 1610612736 | bytes 4466692 | tf_op jit(solution)/shard_map/lever/pallas_call | solution.py:142
  37.6 0.3 collective-permute-done.1.other
  37.9 0.6 backward.1
  38.5 0.0 copy-start.2
  38.5 20.5 %all_to_all.11.parts = f32[32,16,512]{2,1,0:T(8,128)S(1)} all-to-all(f32[32,16,512]{2,1,0:T(8,128)S(1)} %backward.1), channel_id=1, replica_groups=mesh['cmp'=32,'tgt'=4] {'cmp'}, dimensions={0} | all-to-all | bytes 2097152 | tf_op jit(solution)/shard_map/all_to_all | solution.py:190
  59.0 0.0 copy-done.2
  59.0 1.3 %fit.1 = (bf16[256,512]{1,0:T(8,128)(2,1)}, bf16[256,512]{1,0:T(8,128)(2,1)}) custom-call(f32[32,16,512]{2,1,0:T(8,128)S(1)} %all_to_all.11.parts, bf16[256,512]{1,0:T(8,128)(2,1)S(1)} %copy-done.1, bf16[256,512]{1,0:T(8,128)(2,1)S(1)} %copy-done.2, f32[256,512]{1,0:T(8,128)S(1)} %get-tuple-element.13.inverse), custom_call_target="tpu_custom_call" | custom-call | flops 268435456 | bytes 2097152 | tf_op jit(solution)/shard_map/fit/pallas_call | solution.py:142
Async XLA Ops:
  0.6 28.6 %copy-start = (bf16[512,2048]{1,0:T(8,128)(2,1)S(1)}, bf16[512,2048]{1,0:T(8,128)(2,1)}, u32[]{:S(2)}) copy-start(bf16[512,2048]{1,0:T(8,128)(2,1)} %target_basis.3) | copy-start | bytes 6291460
  29.2 4.6 %copy-start.1 = (bf16[256,512]{1,0:T(8,128)(2,1)S(1)}, bf16[256,512]{1,0:T(8,128)(2,1)}, u32[]{:S(2)}) copy-start(bf16[256,512]{1,0:T(8,128)(2,1)} %drug_basis.5) | copy-start | bytes 786436
  29.2 4.6 %copy-start.3 = (f32[2048]{0:T(1024)S(1)}, f32[2048]{0:T(1024)}, u32[]{:S(2)}) copy-start(f32[2048]{0:T(1024)} %param.10) | copy-start | bytes 24580
  29.2 4.6 %copy-start.4 = (f32[512]{0:T(512)S(1)}, f32[512]{0:T(512)}, u32[]{:S(2)}) copy-start(f32[512]{0:T(512)} %param.9) | copy-start | bytes 6148
  29.7 1.4 %collective-permute-start = (f32[16,2048]{1,0:T(8,128)S(1)}, f32[16,2048]{1,0:T(8,128)S(1)}, u32[]{:S(2)}, u32[]{:S(2)}) collective-permute-start(f32[16,2048]{1,0:T(8,128)S(1)} %get-tuple-element.8.mine), channel_id=1, source_target_pairs={{0,1},{1,0},{2,3},{3,2},{4,5},{5,4},{6,7},{7,6},{8,9},{9,8},{10,11... | collective-permute-start | bytes 393224 | tf_op jit(solution)/shard_map/ppermute | solution.py:182
  31.6 6.3 %collective-permute-start.1 = (f32[16,2048]{1,0:T(8,128)S(1)}, f32[16,2048]{1,0:T(8,128)S(1)}, u32[]{:S(2)}, u32[]{:S(2)}) collective-permute-start(f32[16,2048]{1,0:T(8,128)S(1)} %get-tuple-element.9.mine), channel_id=1, source_target_pairs={{0,6},{1,7},{2,4},{3,5},{4,2},{5,3},{6,0},{7,1},{8,14},{9,15},{10,... | collective-permute-start | bytes 393224 | tf_op jit(solution)/shard_map/ppermute | solution.py:185
  38.5 20.5 %copy-start.2 = (bf16[256,512]{1,0:T(8,128)(2,1)S(1)}, bf16[256,512]{1,0:T(8,128)(2,1)}, u32[]{:S(2)}) copy-start(bf16[256,512]{1,0:T(8,128)(2,1)} %activity.3) | copy-start | bytes 786436

commit v5 on v4

--- a/solution.py
+++ b/solution.py
@@ -35,8 +35,17 @@
     return lax.rem(lax.axis_index("tgt"), 2)
 
 
-def crossed():
-    return lax.axis_index("tgt") // 2
+def owners(drug_devices, target_devices):
+    here = range(drug_devices // 2)
+    return [
+        [(2 * place + (low ^ block // 2)) * target_devices + block for low in range(2) for place in here]
+        for block in range(target_devices)
+    ]
+
+
+def owned():
+    place, block = lax.axis_index("cmp"), lax.axis_index("tgt")
+    return (lax.rem(place, 2) ^ (block // 2)) * (lax.axis_size("cmp") // 2) + place // 2
 
 
 def eigen(drug_values, first, rows):
@@ -47,7 +56,7 @@
 
 
 def project(drug_basis, activity, out, basis, values, sems):
-    devices, share, _ = out.shape
+    devices, share, width = out.shape
     copies = [
         pltpu.make_async_copy(drug_basis, basis, sems.at[0]),
         pltpu.make_async_copy(activity, values, sems.at[1]),
@@ -57,9 +66,7 @@
     for copy in copies:
         copy.wait()
     sums = dot(basis[...], values[...], (0, 0))
-    flip = crossed()
-    for k in range(devices):
-        out[jnp.int32(k) ^ flip] = sums[k * share : (k + 1) * share]
+    out[...] = sums.reshape(devices, share, width)
 
 
 def forward(parts, target_basis, out, turned):
@@ -91,8 +98,7 @@
 def lever(drug_values, target_values, ridge, drug_basis, turned_0, turned_1, inverse, weights):
     rank, targets, share = drug_values.shape[1], target_values.shape[1], weights.shape[0]
     offset = ridge[0]
-    first = (lax.axis_index("cmp") ^ crossed()) * share
-    product = eigen(drug_values, first, share) * target_values[...]
+    product = eigen(drug_values, owned() * share, share) * target_values[...]
     weights[...] = product / (product + offset)
     wide = drug_basis[...].astype(jnp.float32)
     squares = halves(wide * wide)
@@ -122,14 +128,11 @@
     of_core(work, turned_0, turned_1)
 
 
-def fit(parts, drug_basis, activity, inverse, fitted, residual, high, low):
-    devices, share, _ = parts.shape
-    flip = crossed()
-    for k in range(devices):
-        rows = pl.ds(k * share, share)
-        high[rows], low[rows] = halves(parts[jnp.int32(k) ^ flip])
+def fit(parts, drug_basis, activity, inverse, fitted, residual):
+    devices, share, width = parts.shape
+    high, low = halves(parts[...].reshape(devices * share, width))
     basis = drug_basis[...]
-    full = dot(basis, high[...]) + dot(basis, low[...])
+    full = dot(basis, high) + dot(basis, low)
     fitted[...] = full.astype(fitted.dtype)
     wide = activity[...].astype(jnp.float32)
     residual[...] = ((wide - full) * inverse[...]).astype(residual.dtype)
@@ -176,7 +179,8 @@
     )
     far = [pltpu.with_memory_space_constraint(x, pltpu.HBM) for x in (drug_basis, activity)]
     sums = call(project, blocks, 2 * compounds * rank * targets_here, scratch, far=(0, 1))(*far)
-    parts = lax.all_to_all(sums, "cmp", 0, 0)
+    groups = owners(drug_devices, target_devices)
+    parts = lax.all_to_all(sums, ("cmp", "tgt"), 0, 0, axis_index_groups=groups)
     flops = 4 * share * targets_here * targets
     coeff, turned_1 = call(forward, (rows, turned), flops)(parts, target_basis)
     other = lax.ppermute(coeff, "tgt", [(i, i ^ 1) for i in range(target_devices)])
@@ -187,9 +191,8 @@
         drug_values[None], target_values[None], ridge, drug_basis, turned_0, turned_1
     )
     back = call(backward, blocks, flops)(coeff, other, weights, turned_0, turned_1)
-    back = lax.all_to_all(back, "cmp", 0, 0)
-    scratch = (pltpu.VMEM((rank, targets_here), bf16),) * 2
-    return call(fit, (output, output), 4 * compounds * rank * targets_here, scratch)(
+    back = lax.all_to_all(back, ("cmp", "tgt"), 0, 0, axis_index_groups=groups)
+    return call(fit, (output, output), 4 * compounds * rank * targets_here)(
         back, drug_basis, activity, inverse
     )
 

time: 60.5 us -> 58.8 us (0.972)
  blocking collectives: 47.5 us -> 45.5 us
    all_to_all x2, blocking collectives: 47.5 us -> 45.5 us  [the longest x1 25.6 us: shards(): parts = lax.all_to_all(sums, ('cmp', 'tgt'), 0, 0, axis_index_groups=groups)]
  transfers between devices with their start and end apart: 2 -> 2, of which waited for: 2 -> 2; matrix products, arithmetic and copies ran while one was open for 0% -> 0% of each run, Pallas kernels for 6% -> 7%
where the time goes in v5:
time: 58.8 us; the launch traced here: 58.2 us
  blocking collectives  45.5 us (77%)
  Pallas kernels  8.22 us (14%)
  starting transfers between devices  2.18 us (4%)
  between operations  1.36 us (2%)
  waiting for transfers between devices  0.96 us (2%)
    all_to_all x1, blocking collectives, shards(): parts = lax.all_to_all(sums, ('cmp', 'tgt'), 0, 0, axis_index_groups=groups)  25.6 us
    all_to_all x1, blocking collectives, shards(): back = lax.all_to_all(back, ('cmp', 'tgt'), 0, 0, axis_index_groups=groups)  19.9 us
    pallas_call x6, Pallas kernels, run(): pl.pallas_call(body, out_shape=outs, in_specs=[pl.BlockSpec(memory_space=...  8.22 us
    ppermute x1, starting transfers between devices, shards(): lax.ppermute(coeff, ('cmp', 'tgt'), [(i, i ^ across) for i in devices])  2.18 us
  transfers between devices with their start and end apart: 2, of which 2 were waited for; matrix products, arithmetic and copies ran while one was open for 0% of the time, Pallas kernels for 7%

profile of v5, /device:TPU:0, one launch (start us, length us, event | category | flops | bytes accessed | tf_op | source)
XLA Modules:
  0.0 58.2 jit_solution(3134451603178388810)
XLA Ops:
  0.6 0.0 copy-start
  0.6 1.5 %project.1 = f32[32,16,512]{2,1,0:T(8,128)S(1)} custom-call(bf16[256,512]{1,0:T(8,128)(2,1)} %drug_basis.5, bf16[256,512]{1,0:T(8,128)(2,1)} %activity.3), custom_call_target="tpu_custom_call" | custom-call | flops 134217728 | bytes 524288 | tf_op jit(solution)/shard_map/project/pallas_call | solution.py:145
  2.2 25.6 %all_to_all.10.parts = f32[32,16,512]{2,1,0:T(8,128)S(1)} all-to-all(f32[32,16,512]{2,1,0:T(8,128)S(1)} %project.1), channel_id=1, replica_groups={{0,8,16,24,32,40,48,56,64,72,80,88,96,104,112,120,4,12,20,28,36,44,52,6..., dimensions={0} | all-to-all | bytes 2097152 | tf_op jit(solution)/shard_map/all_to_all | solution.py:183
  27.8 0.0 copy-done
  27.8 0.0 copy-start.1
  27.8 0.0 copy-start.3
  27.8 0.0 copy-start.4
  27.8 0.5 forward.1
  28.3 0.0 collective-permute-start
  28.9 0.7 %collective-permute-done.other = f32[16,2048]{1,0:T(8,128)S(1)} collective-permute-done((f32[16,2048]{1,0:T(8,128)S(1)}, f32[16,2048]{1,0:T(8,128)S(1)}, u32[]{:S(2)}, u32[]{:S(2)}) %collective-permute-start) | collective-permute-done | bytes 131104 | tf_op jit(solution)/shard_map/ppermute | solution.py:186
  29.6 0.6 %middle.1 = (f32[16,2048]{1,0:T(8,128)S(1)}, bf16[2048,512]{1,0:T(8,128)(2,1)S(1)}) custom-call(f32[16,2048]{1,0:T(8,128)S(1)} %get-tuple-element.8.mine, f32[16,2048]{1,0:T(8,128)S(1)} %collective-permute-done.other, bf16[512,2048]{1,0:T(8,128)(2,1)S(1)} %copy-done), custom_call_target="tpu_custom_call" | custom-call | flops 1048576 | bytes 2359296 | tf_op jit(solution)/shard_map/middle/pallas_call | solution.py:145
  30.2 2.2 %collective-permute-start.1 = (f32[16,2048]{1,0:T(8,128)S(1)}, f32[16,2048]{1,0:T(8,128)S(1)}, u32[]{:S(2)}, u32[]{:S(2)}) collective-permute-start(f32[16,2048]{1,0:T(8,128)S(1)} %get-tuple-element.9.mine), channel_id=1, source_target_pairs={{0,6},{1,7},{2,4},{3,5},{4,2},{5,3},{6,0},{7,1},{8,14},{9,15},{10,... | collective-permute-start | bytes 393224 | tf_op jit(solution)/shard_map/ppermute | solution.py:189
  32.4 0.0 copy-done.1
  32.4 0.0 copy-done.3
  32.4 0.0 copy-done.4
  32.4 3.8 %lever.1 = (f32[256,512]{1,0:T(8,128)S(1)}, f32[16,2048]{1,0:T(8,128)S(1)}) custom-call(f32[1,512]{1,0:T(1,128)S(1)} %bitcast.3, f32[1,2048]{1,0:T(1,128)S(1)} %bitcast.2, f32[1]{0:T(128)S(6)} %copy.8.ridge, bf16[256,512]{1,0:T(8,128)(2,1)S(1)} %copy-done.1, bf16[2048,512]{1,0:T(8,128)(2,1)S(1)} %get-tuple-element.10.turned_0, ...), custom_call_target="tpu_custom_call" | custom-call | flops 1610612736 | bytes 4466692 | tf_op jit(solution)/shard_map/lever/pallas_call | solution.py:145
  36.2 0.3 collective-permute-done.1.other
  36.5 0.6 backward.1
  37.1 0.0 copy-start.2
  37.1 19.9 %all_to_all.11.parts = f32[32,16,512]{2,1,0:T(8,128)S(1)} all-to-all(f32[32,16,512]{2,1,0:T(8,128)S(1)} %backward.1), channel_id=1, replica_groups={{0,8,16,24,32,40,48,56,64,72,80,88,96,104,112,120,4,12,20,28,36,44,52,6..., dimensions={0} | all-to-all | bytes 2097152 | tf_op jit(solution)/shard_map/all_to_all | solution.py:194
  57.0 0.0 copy-done.2
  57.0 1.3 %fit.1 = (bf16[256,512]{1,0:T(8,128)(2,1)}, bf16[256,512]{1,0:T(8,128)(2,1)}) custom-call(f32[32,16,512]{2,1,0:T(8,128)S(1)} %all_to_all.11.parts, bf16[256,512]{1,0:T(8,128)(2,1)S(1)} %copy-done.1, bf16[256,512]{1,0:T(8,128)(2,1)S(1)} %copy-done.2, f32[256,512]{1,0:T(8,128)S(1)} %get-tuple-element.13.inverse), custom_call_target="tpu_custom_call" | custom-call | flops 268435456 | bytes 2097152 | tf_op jit(solution)/shard_map/fit/pallas_call | solution.py:145
Async XLA Ops:
  0.6 27.1 %copy-start = (bf16[512,2048]{1,0:T(8,128)(2,1)S(1)}, bf16[512,2048]{1,0:T(8,128)(2,1)}, u32[]{:S(2)}) copy-start(bf16[512,2048]{1,0:T(8,128)(2,1)} %target_basis.3) | copy-start | bytes 6291460
  27.8 4.6 %copy-start.1 = (bf16[256,512]{1,0:T(8,128)(2,1)S(1)}, bf16[256,512]{1,0:T(8,128)(2,1)}, u32[]{:S(2)}) copy-start(bf16[256,512]{1,0:T(8,128)(2,1)} %drug_basis.5) | copy-start | bytes 786436
  27.8 4.6 %copy-start.3 = (f32[2048]{0:T(1024)S(1)}, f32[2048]{0:T(1024)}, u32[]{:S(2)}) copy-start(f32[2048]{0:T(1024)} %param.10) | copy-start | bytes 24580
  27.8 4.6 %copy-start.4 = (f32[512]{0:T(512)S(1)}, f32[512]{0:T(512)}, u32[]{:S(2)}) copy-start(f32[512]{0:T(512)} %param.9) | copy-start | bytes 6148
  28.3 1.4 %collective-permute-start = (f32[16,2048]{1,0:T(8,128)S(1)}, f32[16,2048]{1,0:T(8,128)S(1)}, u32[]{:S(2)}, u32[]{:S(2)}) collective-permute-start(f32[16,2048]{1,0:T(8,128)S(1)} %get-tuple-element.8.mine), channel_id=1, source_target_pairs={{0,1},{1,0},{2,3},{3,2},{4,5},{5,4},{6,7},{7,6},{8,9},{9,8},{10,11... | collective-permute-start | bytes 393224 | tf_op jit(solution)/shard_map/ppermute | solution.py:186
  30.2 6.3 %collective-permute-start.1 = (f32[16,2048]{1,0:T(8,128)S(1)}, f32[16,2048]{1,0:T(8,128)S(1)}, u32[]{:S(2)}, u32[]{:S(2)}) collective-permute-start(f32[16,2048]{1,0:T(8,128)S(1)} %get-tuple-element.9.mine), channel_id=1, source_target_pairs={{0,6},{1,7},{2,4},{3,5},{4,2},{5,3},{6,0},{7,1},{8,14},{9,15},{10,... | collective-permute-start | bytes 393224 | tf_op jit(solution)/shard_map/ppermute | solution.py:189
  37.1 19.9 %copy-start.2 = (bf16[256,512]{1,0:T(8,128)(2,1)S(1)}, bf16[256,512]{1,0:T(8,128)(2,1)}, u32[]{:S(2)}) copy-start(bf16[256,512]{1,0:T(8,128)(2,1)} %activity.3) | copy-start | bytes 786436

commit v6 on v5

--- a/solution.py
+++ b/solution.py
@@ -6,7 +6,7 @@
 from jax.sharding import PartitionSpec as P
 
 MIB = 1024 * 1024
-PIECES = 2
+PIECES, LATE = 4, 1
 
 
 def halves(x):
@@ -95,28 +95,34 @@
         work(turned_1)
 
 
-def lever(drug_values, target_values, ridge, drug_basis, turned_0, turned_1, inverse, weights):
-    rank, targets, share = drug_values.shape[1], target_values.shape[1], weights.shape[0]
-    offset = ridge[0]
-    product = eigen(drug_values, owned() * share, share) * target_values[...]
-    weights[...] = product / (product + offset)
+def leverage(drug_values, target_values, ridge, drug_basis, turned, pieces):
     wide = drug_basis[...].astype(jnp.float32)
     squares = halves(wide * wide)
-    own = eigen(drug_values, 0, rank)
-
-    def work(turned):
-        step = targets // PIECES
-        total = None
-        for start in range(0, targets, step):
-            some = slice(start, start + step)
-            product = own * target_values[:, some]
-            mixed = dot_pairs(squares, halves(product / (product + offset)))
-            wide = turned[some].astype(jnp.float32)
-            term = dot_pairs(halves(mixed), halves(wide * wide))
-            total = term if total is None else total + term
-        inverse[...] = 1.0 / (1.0 - total)
-
-    of_core(work, turned_0, turned_1)
+    own = eigen(drug_values, 0, drug_values.shape[1])
+    step = target_values.shape[1] // PIECES
+    total = None
+    for piece in pieces:
+        some = slice(piece * step, (piece + 1) * step)
+        product = own * target_values[:, some]
+        mixed = dot_pairs(squares, halves(product / (product + ridge[0])))
+        wide = turned[some].astype(jnp.float32)
+        term = dot_pairs(halves(mixed), halves(wide * wide))
+        total = term if total is None else total + term
+    return total
+
+
+def lever(drug_values, target_values, ridge, drug_basis, turned_0, turned_1, total, weights):
+    values = drug_values, target_values, ridge, drug_basis
+    product = eigen(drug_values, owned() * weights.shape[0], weights.shape[0]) * target_values[...]
+    weights[...] = product / (product + ridge[0])
+
+    @pl.when(core() == 0)
+    def _():
+        total[...] = leverage(*values, turned_0, range(PIECES))
+
+    @pl.when(core() == 1)
+    def _():
+        total[...] = leverage(*values, turned_1, range(PIECES - LATE))
 
 
 def backward(mine, other, weights, turned_0, turned_1, out):
@@ -128,14 +134,21 @@
     of_core(work, turned_0, turned_1)
 
 
-def fit(parts, drug_basis, activity, inverse, fitted, residual):
+def fit(parts, activity, total, drug_values, target_values, ridge, drug_basis, turned_1, fitted, residual, rest):
     devices, share, width = parts.shape
+    rest[...] = total[...]
+
+    @pl.when(core() == 1)
+    def _():
+        late = range(PIECES - LATE, PIECES)
+        rest[...] += leverage(drug_values, target_values, ridge, drug_basis, turned_1, late)
+
     high, low = halves(parts[...].reshape(devices * share, width))
     basis = drug_basis[...]
     full = dot(basis, high) + dot(basis, low)
     fitted[...] = full.astype(fitted.dtype)
     wide = activity[...].astype(jnp.float32)
-    residual[...] = ((wide - full) * inverse[...]).astype(residual.dtype)
+    residual[...] = ((wide - full) / (1.0 - rest[...])).astype(residual.dtype)
 
 
 def call(body, outs, flops, scratch=(), far=(), scalar=()):
@@ -187,13 +200,15 @@
     coeff, turned_0 = call(middle, (rows, turned), targets_here * targets)(coeff, other, target_basis)
     across = target_devices | 2
     other = lax.ppermute(coeff, ("cmp", "tgt"), [(i, i ^ across) for i in devices])
-    inverse, weights = call(lever, (here, rows), 6 * compounds * rank * targets, scalar=(2,))(
-        drug_values[None], target_values[None], ridge, drug_basis, turned_0, turned_1
+    values = (drug_values[None], target_values[None], ridge, drug_basis)
+    total, weights = call(lever, (here, rows), 6 * compounds * rank * targets, scalar=(2,))(
+        *values, turned_0, turned_1
     )
     back = call(backward, blocks, flops)(coeff, other, weights, turned_0, turned_1)
     back = lax.all_to_all(back, ("cmp", "tgt"), 0, 0, axis_index_groups=groups)
-    return call(fit, (output, output), 4 * compounds * rank * targets_here)(
-        back, drug_basis, activity, inverse
+    scratch = (pltpu.VMEM(here.shape, f32),)
+    return call(fit, (output, output), 4 * compounds * rank * targets_here, scratch, scalar=(5,))(
+        back, activity, total, *values, turned_1
     )
 
 

time: 58.8 us -> 58.2 us (0.990)
  blocking collectives: 45.5 us -> 44.8 us
    all_to_all x1, blocking collectives: 19.9 us -> 19.2 us  [shards(): back = lax.all_to_all(back, ('cmp', 'tgt'), 0, 0, axis_index_groups=groups)]
  transfers between devices with their start and end apart: 2 -> 2, of which waited for: 2 -> 1; matrix products, arithmetic and copies ran while one was open for 0% -> 0% of each run, Pallas kernels for 7% -> 7%
where the time goes in v6:
time: 58.2 us; the launch traced here: 57.7 us
  blocking collectives  44.8 us (77%)
  Pallas kernels  8.57 us (15%)
  starting transfers between devices  2.18 us (4%)
  between operations  1.37 us (2%)
  waiting for transfers between devices  0.7 us (1%)
    all_to_all x1, blocking collectives, shards(): parts = lax.all_to_all(sums, ('cmp', 'tgt'), 0, 0, axis_index_groups=groups)  25.6 us
    all_to_all x1, blocking collectives, shards(): back = lax.all_to_all(back, ('cmp', 'tgt'), 0, 0, axis_index_groups=groups)  19.2 us
    pallas_call x6, Pallas kernels, run(): pl.pallas_call(body, out_shape=outs, in_specs=[pl.BlockSpec(memory_space=...  8.57 us
    ppermute x1, starting transfers between devices, shards(): lax.ppermute(coeff, ('cmp', 'tgt'), [(i, i ^ across) for i in devices])  2.18 us
  transfers between devices with their start and end apart: 2, of which 1 were waited for; matrix products, arithmetic and copies ran while one was open for 0% of the time, Pallas kernels for 7%

profile of v6, /device:TPU:0, one launch (start us, length us, event | category | flops | bytes accessed | tf_op | source)
XLA Modules:
  0.0 57.7 jit_solution(11147409194547936658)
XLA Ops:
  0.6 0.0 copy-start
  0.6 1.5 %project.1 = f32[32,16,512]{2,1,0:T(8,128)S(1)} custom-call(bf16[256,512]{1,0:T(8,128)(2,1)} %drug_basis.5, bf16[256,512]{1,0:T(8,128)(2,1)} %activity.3), custom_call_target="tpu_custom_call" | custom-call | flops 134217728 | bytes 524288 | tf_op jit(solution)/shard_map/project/pallas_call | solution.py:158
  2.2 25.6 %all_to_all.10.parts = f32[32,16,512]{2,1,0:T(8,128)S(1)} all-to-all(f32[32,16,512]{2,1,0:T(8,128)S(1)} %project.1), channel_id=1, replica_groups={{0,8,16,24,32,40,48,56,64,72,80,88,96,104,112,120,4,12,20,28,36,44,52,6..., dimensions={0} | all-to-all | bytes 2097152 | tf_op jit(solution)/shard_map/all_to_all | solution.py:196
  27.8 0.0 copy-done
  27.8 0.0 copy-start.1
  27.8 0.0 copy-start.3
  27.8 0.0 copy-start.4
  27.8 0.5 forward.1
  28.3 0.0 collective-permute-start
  28.9 0.7 %collective-permute-done.other = f32[16,2048]{1,0:T(8,128)S(1)} collective-permute-done((f32[16,2048]{1,0:T(8,128)S(1)}, f32[16,2048]{1,0:T(8,128)S(1)}, u32[]{:S(2)}, u32[]{:S(2)}) %collective-permute-start) | collective-permute-done | bytes 131104 | tf_op jit(solution)/shard_map/ppermute | solution.py:199
  29.6 0.6 %middle.1 = (f32[16,2048]{1,0:T(8,128)S(1)}, bf16[2048,512]{1,0:T(8,128)(2,1)S(1)}) custom-call(f32[16,2048]{1,0:T(8,128)S(1)} %get-tuple-element.8.mine, f32[16,2048]{1,0:T(8,128)S(1)} %collective-permute-done.other, bf16[512,2048]{1,0:T(8,128)(2,1)S(1)} %copy-done), custom_call_target="tpu_custom_call" | custom-call | flops 1048576 | bytes 2359296 | tf_op jit(solution)/shard_map/middle/pallas_call | solution.py:158
  30.2 2.2 %collective-permute-start.1 = (f32[16,2048]{1,0:T(8,128)S(1)}, f32[16,2048]{1,0:T(8,128)S(1)}, u32[]{:S(2)}, u32[]{:S(2)}) collective-permute-start(f32[16,2048]{1,0:T(8,128)S(1)} %get-tuple-element.9.mine), channel_id=1, source_target_pairs={{0,6},{1,7},{2,4},{3,5},{4,2},{5,3},{6,0},{7,1},{8,14},{9,15},{10,... | collective-permute-start | bytes 393224 | tf_op jit(solution)/shard_map/ppermute | solution.py:202
  32.4 0.0 copy-done.1
  32.4 0.0 copy-done.3
  32.4 0.0 copy-done.4
  32.4 4.1 %lever.1 = (f32[256,512]{1,0:T(8,128)S(1)}, f32[16,2048]{1,0:T(8,128)S(1)}) custom-call(f32[1,512]{1,0:T(1,128)S(1)} %bitcast.4, f32[1,2048]{1,0:T(1,128)S(1)} %bitcast.2, f32[1]{0:T(128)S(6)} %copy.8.ridge, bf16[256,512]{1,0:T(8,128)(2,1)S(1)} %copy-done.1, bf16[2048,512]{1,0:T(8,128)(2,1)S(1)} %get-tuple-element.10.turned_0, ...), custom_call_target="tpu_custom_call" | custom-call | flops 1610612736 | bytes 4466692 | tf_op jit(solution)/shard_map/lever/pallas_call | solution.py:158
  36.5 0.0 collective-permute-done.1.other
  36.5 0.6 %backward.1 = f32[32,16,512]{2,1,0:T(8,128)S(1)} custom-call(f32[16,2048]{1,0:T(8,128)S(1)} %get-tuple-element.9.mine, f32[16,2048]{1,0:T(8,128)S(1)} %collective-permute-done.1.other, f32[16,2048]{1,0:T(8,128)S(1)} %get-tuple-element.12.weights, bf16[2048,512]{1,0:T(8,128)(2,1)S(1)} %get-tuple-element.10.turned_0, ...), custom_call_target="tpu_custom_call" | custom-call | flops 67108864 | bytes 4587520 | tf_op jit(solution)/shard_map/backward/pallas_call | solution.py:158
  37.1 0.0 copy-start.2
  37.1 19.2 %all_to_all.11.parts = f32[32,16,512]{2,1,0:T(8,128)S(1)} all-to-all(f32[32,16,512]{2,1,0:T(8,128)S(1)} %backward.1), channel_id=1, replica_groups={{0,8,16,24,32,40,48,56,64,72,80,88,96,104,112,120,4,12,20,28,36,44,52,6..., dimensions={0} | all-to-all | bytes 2097152 | tf_op jit(solution)/shard_map/all_to_all | solution.py:208
  56.4 0.0 copy-done.2
  56.4 1.3 %fit.1 = (bf16[256,512]{1,0:T(8,128)(2,1)}, bf16[256,512]{1,0:T(8,128)(2,1)}) custom-call(f32[32,16,512]{2,1,0:T(8,128)S(1)} %all_to_all.11.parts, bf16[256,512]{1,0:T(8,128)(2,1)S(1)} %copy-done.2, f32[256,512]{1,0:T(8,128)S(1)} %get-tuple-element.13.total, f32[1,512]{1,0:T(1,128)S(1)} %bitcast.5, f32[1,2048]{1,0:T(1,128)S(1)} %bitcast.3, f32[1]{0:T(128)S(6)} %copy.8.ridge, ...), custom_call_target="tpu_custom_call" | custom-call | flops 268435456 | bytes 4204548 | tf_op jit(solution)/shard_map/fit/pallas_call | solution.py:158
Async XLA Ops:
  0.6 27.1 %copy-start = (bf16[512,2048]{1,0:T(8,128)(2,1)S(1)}, bf16[512,2048]{1,0:T(8,128)(2,1)}, u32[]{:S(2)}) copy-start(bf16[512,2048]{1,0:T(8,128)(2,1)} %target_basis.3) | copy-start | bytes 6291460
  27.8 4.6 %copy-start.1 = (bf16[256,512]{1,0:T(8,128)(2,1)S(1)}, bf16[256,512]{1,0:T(8,128)(2,1)}, u32[]{:S(2)}) copy-start(bf16[256,512]{1,0:T(8,128)(2,1)} %drug_basis.5) | copy-start | bytes 786436
  27.8 4.6 %copy-start.3 = (f32[2048]{0:T(1024)S(1)}, f32[2048]{0:T(1024)}, u32[]{:S(2)}) copy-start(f32[2048]{0:T(1024)} %param.10) | copy-start | bytes 24580
  27.8 4.6 %copy-start.4 = (f32[512]{0:T(512)S(1)}, f32[512]{0:T(512)}, u32[]{:S(2)}) copy-start(f32[512]{0:T(512)} %param.9) | copy-start | bytes 6148
  28.3 1.4 %collective-permute-start = (f32[16,2048]{1,0:T(8,128)S(1)}, f32[16,2048]{1,0:T(8,128)S(1)}, u32[]{:S(2)}, u32[]{:S(2)}) collective-permute-start(f32[16,2048]{1,0:T(8,128)S(1)} %get-tuple-element.8.mine), channel_id=1, source_target_pairs={{0,1},{1,0},{2,3},{3,2},{4,5},{5,4},{6,7},{7,6},{8,9},{9,8},{10,11... | collective-permute-start | bytes 393224 | tf_op jit(solution)/shard_map/ppermute | solution.py:199
  30.2 6.3 %collective-permute-start.1 = (f32[16,2048]{1,0:T(8,128)S(1)}, f32[16,2048]{1,0:T(8,128)S(1)}, u32[]{:S(2)}, u32[]{:S(2)}) collective-permute-start(f32[16,2048]{1,0:T(8,128)S(1)} %get-tuple-element.9.mine), channel_id=1, source_target_pairs={{0,6},{1,7},{2,4},{3,5},{4,2},{5,3},{6,0},{7,1},{8,14},{9,15},{10,... | collective-permute-start | bytes 393224 | tf_op jit(solution)/shard_map/ppermute | solution.py:202
  37.1 19.2 %copy-start.2 = (bf16[256,512]{1,0:T(8,128)(2,1)S(1)}, bf16[256,512]{1,0:T(8,128)(2,1)}, u32[]{:S(2)}) copy-start(bf16[256,512]{1,0:T(8,128)(2,1)} %activity.3) | copy-start | bytes 786436

commit v7 on v6

--- a/solution.py
+++ b/solution.py
@@ -6,6 +6,8 @@
 from jax.sharding import PartitionSpec as P
 
 MIB = 1024 * 1024
+PLANE, Z = 16, 4
+AHEAD = (2, 1)
 PIECES, LATE = 4, 1
 
 
@@ -35,17 +37,22 @@
     return lax.rem(lax.axis_index("tgt"), 2)
 
 
+def rank_of(place):
+    y, z = place // Z, place % Z
+    return (y + AHEAD[0]) % (PLANE // Z) * Z + (z + AHEAD[1]) % Z
+
+
 def owners(drug_devices, target_devices):
-    here = range(drug_devices // 2)
+    places = sorted(range(drug_devices // 2), key=rank_of)
     return [
-        [(2 * place + (low ^ block // 2)) * target_devices + block for low in range(2) for place in here]
+        [(2 * place + (low ^ block // 2)) * target_devices + block for low in range(2) for place in places]
         for block in range(target_devices)
     ]
 
 
 def owned():
     place, block = lax.axis_index("cmp"), lax.axis_index("tgt")
-    return (lax.rem(place, 2) ^ (block // 2)) * (lax.axis_size("cmp") // 2) + place // 2
+    return (lax.rem(place, 2) ^ (block // 2)) * PLANE + rank_of(place // 2)
 
 
 def eigen(drug_values, first, rows):

time: 58.2 us -> 55.9 us (0.960)
  blocking collectives: 44.8 us -> 42.6 us
    all_to_all x1, blocking collectives: 25.6 us -> 23.2 us  [shards(): parts = lax.all_to_all(sums, ('cmp', 'tgt'), 0, 0, axis_index_groups=groups)]
where the time goes in v7:
time: 55.9 us; the launch traced here: 55.7 us
  blocking collectives  42.6 us (76%)
  Pallas kernels  8.58 us (15%)
  starting transfers between devices  2.41 us (4%)
  between operations  1.37 us (2%)
  waiting for transfers between devices  0.7 us (1%)
    all_to_all x1, blocking collectives, shards(): parts = lax.all_to_all(sums, ('cmp', 'tgt'), 0, 0, axis_index_groups=groups)  23.2 us
    all_to_all x1, blocking collectives, shards(): back = lax.all_to_all(back, ('cmp', 'tgt'), 0, 0, axis_index_groups=groups)  19.4 us
    pallas_call x6, Pallas kernels, run(): pl.pallas_call(body, out_shape=outs, in_specs=[pl.BlockSpec(memory_space=...  8.58 us
    ppermute x1, starting transfers between devices, shards(): lax.ppermute(coeff, ('cmp', 'tgt'), [(i, i ^ across) for i in devices])  2.41 us
  transfers between devices with their start and end apart: 2, of which 1 were waited for; matrix products, arithmetic and copies ran while one was open for 0% of the time, Pallas kernels for 7%

profile of v7, /device:TPU:0, one launch (start us, length us, event | category | flops | bytes accessed | tf_op | source)
XLA Modules:
  0.0 55.7 jit_solution(5165358415019834902)
XLA Ops:
  0.6 0.0 copy-start
  0.6 1.5 %project.1 = f32[32,16,512]{2,1,0:T(8,128)S(1)} custom-call(bf16[256,512]{1,0:T(8,128)(2,1)} %drug_basis.5, bf16[256,512]{1,0:T(8,128)(2,1)} %activity.3), custom_call_target="tpu_custom_call" | custom-call | flops 134217728 | bytes 524288 | tf_op jit(solution)/shard_map/project/pallas_call | solution.py:165
  2.2 23.2 %all_to_all.10.parts = f32[32,16,512]{2,1,0:T(8,128)S(1)} all-to-all(f32[32,16,512]{2,1,0:T(8,128)S(1)} %project.1), channel_id=1, replica_groups={{88,64,72,80,120,96,104,112,24,0,8,16,56,32,40,48,92,68,76,84,124,100,1..., dimensions={0} | all-to-all | bytes 2097152 | tf_op jit(solution)/shard_map/all_to_all | solution.py:203
  25.4 0.0 copy-done
  25.4 0.0 copy-start.1
  25.4 0.0 copy-start.3
  25.4 0.0 copy-start.4
  25.4 0.5 forward.1
  25.9 0.0 collective-permute-start
  26.5 0.7 %collective-permute-done.other = f32[16,2048]{1,0:T(8,128)S(1)} collective-permute-done((f32[16,2048]{1,0:T(8,128)S(1)}, f32[16,2048]{1,0:T(8,128)S(1)}, u32[]{:S(2)}, u32[]{:S(2)}) %collective-permute-start) | collective-permute-done | bytes 131104 | tf_op jit(solution)/shard_map/ppermute | solution.py:206
  27.2 0.6 %middle.1 = (f32[16,2048]{1,0:T(8,128)S(1)}, bf16[2048,512]{1,0:T(8,128)(2,1)S(1)}) custom-call(f32[16,2048]{1,0:T(8,128)S(1)} %get-tuple-element.8.mine, f32[16,2048]{1,0:T(8,128)S(1)} %collective-permute-done.other, bf16[512,2048]{1,0:T(8,128)(2,1)S(1)} %copy-done), custom_call_target="tpu_custom_call" | custom-call | flops 1048576 | bytes 2359296 | tf_op jit(solution)/shard_map/middle/pallas_call | solution.py:165
  27.8 2.4 %collective-permute-start.1 = (f32[16,2048]{1,0:T(8,128)S(1)}, f32[16,2048]{1,0:T(8,128)S(1)}, u32[]{:S(2)}, u32[]{:S(2)}) collective-permute-start(f32[16,2048]{1,0:T(8,128)S(1)} %get-tuple-element.9.mine), channel_id=1, source_target_pairs={{0,6},{1,7},{2,4},{3,5},{4,2},{5,3},{6,0},{7,1},{8,14},{9,15},{10,... | collective-permute-start | bytes 393224 | tf_op jit(solution)/shard_map/ppermute | solution.py:209
  30.2 0.0 copy-done.1
  30.2 0.0 copy-done.3
  30.2 0.0 copy-done.4
  30.2 4.1 %lever.1 = (f32[256,512]{1,0:T(8,128)S(1)}, f32[16,2048]{1,0:T(8,128)S(1)}) custom-call(f32[1,512]{1,0:T(1,128)S(1)} %bitcast.4, f32[1,2048]{1,0:T(1,128)S(1)} %bitcast.2, f32[1]{0:T(128)S(6)} %copy.8.ridge, bf16[256,512]{1,0:T(8,128)(2,1)S(1)} %copy-done.1, bf16[2048,512]{1,0:T(8,128)(2,1)S(1)} %get-tuple-element.10.turned_0, ...), custom_call_target="tpu_custom_call" | custom-call | flops 1610612736 | bytes 4466692 | tf_op jit(solution)/shard_map/lever/pallas_call | solution.py:165
  34.4 0.0 collective-permute-done.1.other
  34.4 0.6 %backward.1 = f32[32,16,512]{2,1,0:T(8,128)S(1)} custom-call(f32[16,2048]{1,0:T(8,128)S(1)} %get-tuple-element.9.mine, f32[16,2048]{1,0:T(8,128)S(1)} %collective-permute-done.1.other, f32[16,2048]{1,0:T(8,128)S(1)} %get-tuple-element.12.weights, bf16[2048,512]{1,0:T(8,128)(2,1)S(1)} %get-tuple-element.10.turned_0, ...), custom_call_target="tpu_custom_call" | custom-call | flops 67108864 | bytes 4587520 | tf_op jit(solution)/shard_map/backward/pallas_call | solution.py:165
  35.0 0.0 copy-start.2
  35.0 19.4 %all_to_all.11.parts = f32[32,16,512]{2,1,0:T(8,128)S(1)} all-to-all(f32[32,16,512]{2,1,0:T(8,128)S(1)} %backward.1), channel_id=1, replica_groups={{88,64,72,80,120,96,104,112,24,0,8,16,56,32,40,48,92,68,76,84,124,100,1..., dimensions={0} | all-to-all | bytes 2097152 | tf_op jit(solution)/shard_map/all_to_all | solution.py:215
  54.4 0.0 copy-done.2
  54.4 1.3 %fit.1 = (bf16[256,512]{1,0:T(8,128)(2,1)}, bf16[256,512]{1,0:T(8,128)(2,1)}) custom-call(f32[32,16,512]{2,1,0:T(8,128)S(1)} %all_to_all.11.parts, bf16[256,512]{1,0:T(8,128)(2,1)S(1)} %copy-done.2, f32[256,512]{1,0:T(8,128)S(1)} %get-tuple-element.13.total, f32[1,512]{1,0:T(1,128)S(1)} %bitcast.5, f32[1,2048]{1,0:T(1,128)S(1)} %bitcast.3, f32[1]{0:T(128)S(6)} %copy.8.ridge, ...), custom_call_target="tpu_custom_call" | custom-call | flops 268435456 | bytes 4204548 | tf_op jit(solution)/shard_map/fit/pallas_call | solution.py:165
Async XLA Ops:
  0.6 24.7 %copy-start = (bf16[512,2048]{1,0:T(8,128)(2,1)S(1)}, bf16[512,2048]{1,0:T(8,128)(2,1)}, u32[]{:S(2)}) copy-start(bf16[512,2048]{1,0:T(8,128)(2,1)} %target_basis.3) | copy-start | bytes 6291460
  25.4 4.9 %copy-start.1 = (bf16[256,512]{1,0:T(8,128)(2,1)S(1)}, bf16[256,512]{1,0:T(8,128)(2,1)}, u32[]{:S(2)}) copy-start(bf16[256,512]{1,0:T(8,128)(2,1)} %drug_basis.5) | copy-start | bytes 786436
  25.4 4.9 %copy-start.3 = (f32[2048]{0:T(1024)S(1)}, f32[2048]{0:T(1024)}, u32[]{:S(2)}) copy-start(f32[2048]{0:T(1024)} %param.10) | copy-start | bytes 24580
  25.4 4.9 %copy-start.4 = (f32[512]{0:T(512)S(1)}, f32[512]{0:T(512)}, u32[]{:S(2)}) copy-start(f32[512]{0:T(512)} %param.9) | copy-start | bytes 6148
  25.9 1.4 %collective-permute-start = (f32[16,2048]{1,0:T(8,128)S(1)}, f32[16,2048]{1,0:T(8,128)S(1)}, u32[]{:S(2)}, u32[]{:S(2)}) collective-permute-start(f32[16,2048]{1,0:T(8,128)S(1)} %get-tuple-element.8.mine), channel_id=1, source_target_pairs={{0,1},{1,0},{2,3},{3,2},{4,5},{5,4},{6,7},{7,6},{8,9},{9,8},{10,11... | collective-permute-start | bytes 393224 | tf_op jit(solution)/shard_map/ppermute | solution.py:206
  27.8 6.5 %collective-permute-start.1 = (f32[16,2048]{1,0:T(8,128)S(1)}, f32[16,2048]{1,0:T(8,128)S(1)}, u32[]{:S(2)}, u32[]{:S(2)}) collective-permute-start(f32[16,2048]{1,0:T(8,128)S(1)} %get-tuple-element.9.mine), channel_id=1, source_target_pairs={{0,6},{1,7},{2,4},{3,5},{4,2},{5,3},{6,0},{7,1},{8,14},{9,15},{10,... | collective-permute-start | bytes 393224 | tf_op jit(solution)/shard_map/ppermute | solution.py:209
  35.0 19.4 %copy-start.2 = (bf16[256,512]{1,0:T(8,128)(2,1)S(1)}, bf16[256,512]{1,0:T(8,128)(2,1)}, u32[]{:S(2)}) copy-start(bf16[256,512]{1,0:T(8,128)(2,1)} %activity.3) | copy-start | bytes 786436

commit v8 on v7

--- a/solution.py
+++ b/solution.py
@@ -8,7 +8,7 @@
 MIB = 1024 * 1024
 PLANE, Z = 16, 4
 AHEAD = (2, 1)
-PIECES, LATE = 4, 1
+PIECES, LATE = 4, 2
 
 
 def halves(x):

time: 55.9 us -> 55.8 us (level)
  no operation moved by 1% of the time
where the time goes in v8:
time: 55.8 us; the launch traced here: 55.4 us
  blocking collectives  42.4 us (76%)
  Pallas kernels  8.58 us (15%)
  starting transfers between devices  2.41 us (4%)
  between operations  1.37 us (2%)
  waiting for transfers between devices  0.7 us (1%)
    all_to_all x1, blocking collectives, shards(): parts = lax.all_to_all(sums, ('cmp', 'tgt'), 0, 0, axis_index_groups=groups)  23.2 us
    all_to_all x1, blocking collectives, shards(): back = lax.all_to_all(back, ('cmp', 'tgt'), 0, 0, axis_index_groups=groups)  19.1 us
    pallas_call x6, Pallas kernels, run(): pl.pallas_call(body, out_shape=outs, in_specs=[pl.BlockSpec(memory_space=...  8.58 us
    ppermute x1, starting transfers between devices, shards(): lax.ppermute(coeff, ('cmp', 'tgt'), [(i, i ^ across) for i in devices])  2.41 us
  transfers between devices with their start and end apart: 2, of which 1 were waited for; matrix products, arithmetic and copies ran while one was open for 0% of the time, Pallas kernels for 7%

profile of v8, /device:TPU:0, one launch (start us, length us, event | category | flops | bytes accessed | tf_op | source)
XLA Modules:
  0.0 55.4 jit_solution(14382068370185980644)
XLA Ops:
  0.6 0.0 copy-start
  0.6 1.5 %project.1 = f32[32,16,512]{2,1,0:T(8,128)S(1)} custom-call(bf16[256,512]{1,0:T(8,128)(2,1)} %drug_basis.5, bf16[256,512]{1,0:T(8,128)(2,1)} %activity.3), custom_call_target="tpu_custom_call" | custom-call | flops 134217728 | bytes 524288 | tf_op jit(solution)/shard_map/project/pallas_call | solution.py:165
  2.2 23.2 %all_to_all.10.parts = f32[32,16,512]{2,1,0:T(8,128)S(1)} all-to-all(f32[32,16,512]{2,1,0:T(8,128)S(1)} %project.1), channel_id=1, replica_groups={{88,64,72,80,120,96,104,112,24,0,8,16,56,32,40,48,92,68,76,84,124,100,1..., dimensions={0} | all-to-all | bytes 2097152 | tf_op jit(solution)/shard_map/all_to_all | solution.py:203
  25.4 0.0 copy-done
  25.4 0.0 copy-start.1
  25.4 0.0 copy-start.3
  25.4 0.0 copy-start.4
  25.4 0.5 forward.1
  25.9 0.0 collective-permute-start
  26.5 0.7 %collective-permute-done.other = f32[16,2048]{1,0:T(8,128)S(1)} collective-permute-done((f32[16,2048]{1,0:T(8,128)S(1)}, f32[16,2048]{1,0:T(8,128)S(1)}, u32[]{:S(2)}, u32[]{:S(2)}) %collective-permute-start) | collective-permute-done | bytes 131104 | tf_op jit(solution)/shard_map/ppermute | solution.py:206
  27.2 0.6 %middle.1 = (f32[16,2048]{1,0:T(8,128)S(1)}, bf16[2048,512]{1,0:T(8,128)(2,1)S(1)}) custom-call(f32[16,2048]{1,0:T(8,128)S(1)} %get-tuple-element.8.mine, f32[16,2048]{1,0:T(8,128)S(1)} %collective-permute-done.other, bf16[512,2048]{1,0:T(8,128)(2,1)S(1)} %copy-done), custom_call_target="tpu_custom_call" | custom-call | flops 1048576 | bytes 2359296 | tf_op jit(solution)/shard_map/middle/pallas_call | solution.py:165
  27.8 2.4 %collective-permute-start.1 = (f32[16,2048]{1,0:T(8,128)S(1)}, f32[16,2048]{1,0:T(8,128)S(1)}, u32[]{:S(2)}, u32[]{:S(2)}) collective-permute-start(f32[16,2048]{1,0:T(8,128)S(1)} %get-tuple-element.9.mine), channel_id=1, source_target_pairs={{0,6},{1,7},{2,4},{3,5},{4,2},{5,3},{6,0},{7,1},{8,14},{9,15},{10,... | collective-permute-start | bytes 393224 | tf_op jit(solution)/shard_map/ppermute | solution.py:209
  30.2 0.0 copy-done.1
  30.2 0.0 copy-done.3
  30.2 0.0 copy-done.4
  30.2 4.1 %lever.1 = (f32[256,512]{1,0:T(8,128)S(1)}, f32[16,2048]{1,0:T(8,128)S(1)}) custom-call(f32[1,512]{1,0:T(1,128)S(1)} %bitcast.4, f32[1,2048]{1,0:T(1,128)S(1)} %bitcast.2, f32[1]{0:T(128)S(6)} %copy.8.ridge, bf16[256,512]{1,0:T(8,128)(2,1)S(1)} %copy-done.1, bf16[2048,512]{1,0:T(8,128)(2,1)S(1)} %get-tuple-element.10.turned_0, ...), custom_call_target="tpu_custom_call" | custom-call | flops 1610612736 | bytes 4466692 | tf_op jit(solution)/shard_map/lever/pallas_call | solution.py:165
  34.4 0.0 collective-permute-done.1.other
  34.4 0.6 %backward.1 = f32[32,16,512]{2,1,0:T(8,128)S(1)} custom-call(f32[16,2048]{1,0:T(8,128)S(1)} %get-tuple-element.9.mine, f32[16,2048]{1,0:T(8,128)S(1)} %collective-permute-done.1.other, f32[16,2048]{1,0:T(8,128)S(1)} %get-tuple-element.12.weights, bf16[2048,512]{1,0:T(8,128)(2,1)S(1)} %get-tuple-element.10.turned_0, ...), custom_call_target="tpu_custom_call" | custom-call | flops 67108864 | bytes 4587520 | tf_op jit(solution)/shard_map/backward/pallas_call | solution.py:165
  35.0 0.0 copy-start.2
  35.0 19.1 %all_to_all.11.parts = f32[32,16,512]{2,1,0:T(8,128)S(1)} all-to-all(f32[32,16,512]{2,1,0:T(8,128)S(1)} %backward.1), channel_id=1, replica_groups={{88,64,72,80,120,96,104,112,24,0,8,16,56,32,40,48,92,68,76,84,124,100,1..., dimensions={0} | all-to-all | bytes 2097152 | tf_op jit(solution)/shard_map/all_to_all | solution.py:215
  54.1 0.0 copy-done.2
  54.1 1.3 %fit.1 = (bf16[256,512]{1,0:T(8,128)(2,1)}, bf16[256,512]{1,0:T(8,128)(2,1)}) custom-call(f32[32,16,512]{2,1,0:T(8,128)S(1)} %all_to_all.11.parts, bf16[256,512]{1,0:T(8,128)(2,1)S(1)} %copy-done.2, f32[256,512]{1,0:T(8,128)S(1)} %get-tuple-element.13.total, f32[1,512]{1,0:T(1,128)S(1)} %bitcast.5, f32[1,2048]{1,0:T(1,128)S(1)} %bitcast.3, f32[1]{0:T(128)S(6)} %copy.8.ridge, ...), custom_call_target="tpu_custom_call" | custom-call | flops 268435456 | bytes 4204548 | tf_op jit(solution)/shard_map/fit/pallas_call | solution.py:165
Async XLA Ops:
  0.6 24.7 %copy-start = (bf16[512,2048]{1,0:T(8,128)(2,1)S(1)}, bf16[512,2048]{1,0:T(8,128)(2,1)}, u32[]{:S(2)}) copy-start(bf16[512,2048]{1,0:T(8,128)(2,1)} %target_basis.3) | copy-start | bytes 6291460
  25.4 4.9 %copy-start.1 = (bf16[256,512]{1,0:T(8,128)(2,1)S(1)}, bf16[256,512]{1,0:T(8,128)(2,1)}, u32[]{:S(2)}) copy-start(bf16[256,512]{1,0:T(8,128)(2,1)} %drug_basis.5) | copy-start | bytes 786436
  25.4 4.9 %copy-start.3 = (f32[2048]{0:T(1024)S(1)}, f32[2048]{0:T(1024)}, u32[]{:S(2)}) copy-start(f32[2048]{0:T(1024)} %param.10) | copy-start | bytes 24580
  25.4 4.9 %copy-start.4 = (f32[512]{0:T(512)S(1)}, f32[512]{0:T(512)}, u32[]{:S(2)}) copy-start(f32[512]{0:T(512)} %param.9) | copy-start | bytes 6148
  25.9 1.4 %collective-permute-start = (f32[16,2048]{1,0:T(8,128)S(1)}, f32[16,2048]{1,0:T(8,128)S(1)}, u32[]{:S(2)}, u32[]{:S(2)}) collective-permute-start(f32[16,2048]{1,0:T(8,128)S(1)} %get-tuple-element.8.mine), channel_id=1, source_target_pairs={{0,1},{1,0},{2,3},{3,2},{4,5},{5,4},{6,7},{7,6},{8,9},{9,8},{10,11... | collective-permute-start | bytes 393224 | tf_op jit(solution)/shard_map/ppermute | solution.py:206
  27.8 6.5 %collective-permute-start.1 = (f32[16,2048]{1,0:T(8,128)S(1)}, f32[16,2048]{1,0:T(8,128)S(1)}, u32[]{:S(2)}, u32[]{:S(2)}) collective-permute-start(f32[16,2048]{1,0:T(8,128)S(1)} %get-tuple-element.9.mine), channel_id=1, source_target_pairs={{0,6},{1,7},{2,4},{3,5},{4,2},{5,3},{6,0},{7,1},{8,14},{9,15},{10,... | collective-permute-start | bytes 393224 | tf_op jit(solution)/shard_map/ppermute | solution.py:209
  35.0 19.2 %copy-start.2 = (bf16[256,512]{1,0:T(8,128)(2,1)S(1)}, bf16[256,512]{1,0:T(8,128)(2,1)}, u32[]{:S(2)}) copy-start(bf16[256,512]{1,0:T(8,128)(2,1)} %activity.3) | copy-start | bytes 786436

commit v9 on v8

--- a/solution.py
+++ b/solution.py
@@ -8,7 +8,7 @@
 MIB = 1024 * 1024
 PLANE, Z = 16, 4
 AHEAD = (2, 1)
-PIECES, LATE = 4, 2
+PIECES, LATE = 2, 1
 
 
 def halves(x):

time: 55.8 us -> 55.9 us (level)
  no operation moved by 1% of the time
where the time goes in v9:
time: 55.9 us; the launch traced here: 55.4 us
  blocking collectives  42.6 us (76%)
  Pallas kernels  8.3 us (15%)
  starting transfers between devices  2.41 us (4%)
  between operations  1.37 us (2%)
  waiting for transfers between devices  0.7 us (1%)
    all_to_all x1, blocking collectives, shards(): parts = lax.all_to_all(sums, ('cmp', 'tgt'), 0, 0, axis_index_groups=groups)  23.2 us
    all_to_all x1, blocking collectives, shards(): back = lax.all_to_all(back, ('cmp', 'tgt'), 0, 0, axis_index_groups=groups)  19.4 us
    pallas_call x6, Pallas kernels, run(): pl.pallas_call(body, out_shape=outs, in_specs=[pl.BlockSpec(memory_space=...  8.3 us
    ppermute x1, starting transfers between devices, shards(): lax.ppermute(coeff, ('cmp', 'tgt'), [(i, i ^ across) for i in devices])  2.41 us
  transfers between devices with their start and end apart: 2, of which 1 were waited for; matrix products, arithmetic and copies ran while one was open for 0% of the time, Pallas kernels for 7%

profile of v9, /device:TPU:0, one launch (start us, length us, event | category | flops | bytes accessed | tf_op | source)
XLA Modules:
  0.0 55.4 jit_solution(8931904354852958971)
XLA Ops:
  0.6 0.0 copy-start
  0.6 1.5 %project.1 = f32[32,16,512]{2,1,0:T(8,128)S(1)} custom-call(bf16[256,512]{1,0:T(8,128)(2,1)} %drug_basis.5, bf16[256,512]{1,0:T(8,128)(2,1)} %activity.3), custom_call_target="tpu_custom_call" | custom-call | flops 134217728 | bytes 524288 | tf_op jit(solution)/shard_map/project/pallas_call | solution.py:165
  2.2 23.2 %all_to_all.10.parts = f32[32,16,512]{2,1,0:T(8,128)S(1)} all-to-all(f32[32,16,512]{2,1,0:T(8,128)S(1)} %project.1), channel_id=1, replica_groups={{88,64,72,80,120,96,104,112,24,0,8,16,56,32,40,48,92,68,76,84,124,100,1..., dimensions={0} | all-to-all | bytes 2097152 | tf_op jit(solution)/shard_map/all_to_all | solution.py:203
  25.4 0.0 copy-done
  25.4 0.0 copy-start.1
  25.4 0.0 copy-start.3
  25.4 0.0 copy-start.4
  25.4 0.5 forward.1
  25.9 0.0 collective-permute-start
  26.5 0.7 %collective-permute-done.other = f32[16,2048]{1,0:T(8,128)S(1)} collective-permute-done((f32[16,2048]{1,0:T(8,128)S(1)}, f32[16,2048]{1,0:T(8,128)S(1)}, u32[]{:S(2)}, u32[]{:S(2)}) %collective-permute-start) | collective-permute-done | bytes 131104 | tf_op jit(solution)/shard_map/ppermute | solution.py:206
  27.2 0.6 %middle.1 = (f32[16,2048]{1,0:T(8,128)S(1)}, bf16[2048,512]{1,0:T(8,128)(2,1)S(1)}) custom-call(f32[16,2048]{1,0:T(8,128)S(1)} %get-tuple-element.8.mine, f32[16,2048]{1,0:T(8,128)S(1)} %collective-permute-done.other, bf16[512,2048]{1,0:T(8,128)(2,1)S(1)} %copy-done), custom_call_target="tpu_custom_call" | custom-call | flops 1048576 | bytes 2359296 | tf_op jit(solution)/shard_map/middle/pallas_call | solution.py:165
  27.8 2.4 %collective-permute-start.1 = (f32[16,2048]{1,0:T(8,128)S(1)}, f32[16,2048]{1,0:T(8,128)S(1)}, u32[]{:S(2)}, u32[]{:S(2)}) collective-permute-start(f32[16,2048]{1,0:T(8,128)S(1)} %get-tuple-element.9.mine), channel_id=1, source_target_pairs={{0,6},{1,7},{2,4},{3,5},{4,2},{5,3},{6,0},{7,1},{8,14},{9,15},{10,... | collective-permute-start | bytes 393224 | tf_op jit(solution)/shard_map/ppermute | solution.py:209
  30.2 0.0 copy-done.1
  30.2 0.0 copy-done.3
  30.2 0.0 copy-done.4
  30.2 3.8 %lever.1 = (f32[256,512]{1,0:T(8,128)S(1)}, f32[16,2048]{1,0:T(8,128)S(1)}) custom-call(f32[1,512]{1,0:T(1,128)S(1)} %bitcast.4, f32[1,2048]{1,0:T(1,128)S(1)} %bitcast.2, f32[1]{0:T(128)S(6)} %copy.8.ridge, bf16[256,512]{1,0:T(8,128)(2,1)S(1)} %copy-done.1, bf16[2048,512]{1,0:T(8,128)(2,1)S(1)} %get-tuple-element.10.turned_0, ...), custom_call_target="tpu_custom_call" | custom-call | flops 1610612736 | bytes 4466692 | tf_op jit(solution)/shard_map/lever/pallas_call | solution.py:165
  34.1 0.0 collective-permute-done.1.other
  34.1 0.6 %backward.1 = f32[32,16,512]{2,1,0:T(8,128)S(1)} custom-call(f32[16,2048]{1,0:T(8,128)S(1)} %get-tuple-element.9.mine, f32[16,2048]{1,0:T(8,128)S(1)} %collective-permute-done.1.other, f32[16,2048]{1,0:T(8,128)S(1)} %get-tuple-element.12.weights, bf16[2048,512]{1,0:T(8,128)(2,1)S(1)} %get-tuple-element.10.turned_0, ...), custom_call_target="tpu_custom_call" | custom-call | flops 67108864 | bytes 4587520 | tf_op jit(solution)/shard_map/backward/pallas_call | solution.py:165
  34.7 0.0 copy-start.2
  34.7 19.4 %all_to_all.11.parts = f32[32,16,512]{2,1,0:T(8,128)S(1)} all-to-all(f32[32,16,512]{2,1,0:T(8,128)S(1)} %backward.1), channel_id=1, replica_groups={{88,64,72,80,120,96,104,112,24,0,8,16,56,32,40,48,92,68,76,84,124,100,1..., dimensions={0} | all-to-all | bytes 2097152 | tf_op jit(solution)/shard_map/all_to_all | solution.py:215
  54.1 0.0 copy-done.2
  54.1 1.3 %fit.1 = (bf16[256,512]{1,0:T(8,128)(2,1)}, bf16[256,512]{1,0:T(8,128)(2,1)}) custom-call(f32[32,16,512]{2,1,0:T(8,128)S(1)} %all_to_all.11.parts, bf16[256,512]{1,0:T(8,128)(2,1)S(1)} %copy-done.2, f32[256,512]{1,0:T(8,128)S(1)} %get-tuple-element.13.total, f32[1,512]{1,0:T(1,128)S(1)} %bitcast.5, f32[1,2048]{1,0:T(1,128)S(1)} %bitcast.3, f32[1]{0:T(128)S(6)} %copy.8.ridge, ...), custom_call_target="tpu_custom_call" | custom-call | flops 268435456 | bytes 4204548 | tf_op jit(solution)/shard_map/fit/pallas_call | solution.py:165
Async XLA Ops:
  0.6 24.7 %copy-start = (bf16[512,2048]{1,0:T(8,128)(2,1)S(1)}, bf16[512,2048]{1,0:T(8,128)(2,1)}, u32[]{:S(2)}) copy-start(bf16[512,2048]{1,0:T(8,128)(2,1)} %target_basis.3) | copy-start | bytes 6291460
  25.4 4.9 %copy-start.1 = (bf16[256,512]{1,0:T(8,128)(2,1)S(1)}, bf16[256,512]{1,0:T(8,128)(2,1)}, u32[]{:S(2)}) copy-start(bf16[256,512]{1,0:T(8,128)(2,1)} %drug_basis.5) | copy-start | bytes 786436
  25.4 4.9 %copy-start.3 = (f32[2048]{0:T(1024)S(1)}, f32[2048]{0:T(1024)}, u32[]{:S(2)}) copy-start(f32[2048]{0:T(1024)} %param.10) | copy-start | bytes 24580
  25.4 4.9 %copy-start.4 = (f32[512]{0:T(512)S(1)}, f32[512]{0:T(512)}, u32[]{:S(2)}) copy-start(f32[512]{0:T(512)} %param.9) | copy-start | bytes 6148
  25.9 1.4 %collective-permute-start = (f32[16,2048]{1,0:T(8,128)S(1)}, f32[16,2048]{1,0:T(8,128)S(1)}, u32[]{:S(2)}, u32[]{:S(2)}) collective-permute-start(f32[16,2048]{1,0:T(8,128)S(1)} %get-tuple-element.8.mine), channel_id=1, source_target_pairs={{0,1},{1,0},{2,3},{3,2},{4,5},{5,4},{6,7},{7,6},{8,9},{9,8},{10,11... | collective-permute-start | bytes 393224 | tf_op jit(solution)/shard_map/ppermute | solution.py:206
  27.8 6.3 %collective-permute-start.1 = (f32[16,2048]{1,0:T(8,128)S(1)}, f32[16,2048]{1,0:T(8,128)S(1)}, u32[]{:S(2)}, u32[]{:S(2)}) collective-permute-start(f32[16,2048]{1,0:T(8,128)S(1)} %get-tuple-element.9.mine), channel_id=1, source_target_pairs={{0,6},{1,7},{2,4},{3,5},{4,2},{5,3},{6,0},{7,1},{8,14},{9,15},{10,... | collective-permute-start | bytes 393224 | tf_op jit(solution)/shard_map/ppermute | solution.py:209
  34.7 19.4 %copy-start.2 = (bf16[256,512]{1,0:T(8,128)(2,1)S(1)}, bf16[256,512]{1,0:T(8,128)(2,1)}, u32[]{:S(2)}) copy-start(bf16[256,512]{1,0:T(8,128)(2,1)} %activity.3) | copy-start | bytes 786436

commit v10 on v8

--- a/solution.py
+++ b/solution.py
@@ -7,7 +7,7 @@
 
 MIB = 1024 * 1024
 PLANE, Z = 16, 4
-AHEAD = (2, 1)
+AHEAD = (2, 3)
 PIECES, LATE = 4, 2
 
 
@@ -39,7 +39,7 @@
 
 def rank_of(place):
     y, z = place // Z, place % Z
-    return (y + AHEAD[0]) % (PLANE // Z) * Z + (z + AHEAD[1]) % Z
+    return (AHEAD[0] - y) % (PLANE // Z) * Z + (AHEAD[1] - z) % Z
 
 
 def owners(drug_devices, target_devices):

time: 55.8 us -> 55.7 us (level)
  no operation moved by 1% of the time
where the time goes in v10:
time: 55.7 us; the launch traced here: 55.5 us
  blocking collectives  42.6 us (76%)
  Pallas kernels  8.58 us (15%)
  starting transfers between devices  2.23 us (4%)
  between operations  1.37 us (2%)
  waiting for transfers between devices  0.7 us (1%)
    all_to_all x1, blocking collectives, shards(): parts = lax.all_to_all(sums, ('cmp', 'tgt'), 0, 0, axis_index_groups=groups)  23.6 us
    all_to_all x1, blocking collectives, shards(): back = lax.all_to_all(back, ('cmp', 'tgt'), 0, 0, axis_index_groups=groups)  19 us
    pallas_call x6, Pallas kernels, run(): pl.pallas_call(body, out_shape=outs, in_specs=[pl.BlockSpec(memory_space=...  8.58 us
    ppermute x1, starting transfers between devices, shards(): lax.ppermute(coeff, ('cmp', 'tgt'), [(i, i ^ across) for i in devices])  2.23 us
  transfers between devices with their start and end apart: 2, of which 1 were waited for; matrix products, arithmetic and copies ran while one was open for 0% of the time, Pallas kernels for 7%

profile of v10, /device:TPU:0, one launch (start us, length us, event | category | flops | bytes accessed | tf_op | source)
XLA Modules:
  0.0 55.5 jit_solution(13684131894535222867)
XLA Ops:
  0.6 0.0 copy-start
  0.6 1.5 %project.1 = f32[32,16,512]{2,1,0:T(8,128)S(1)} custom-call(bf16[256,512]{1,0:T(8,128)(2,1)} %drug_basis.5, bf16[256,512]{1,0:T(8,128)(2,1)} %activity.3), custom_call_target="tpu_custom_call" | custom-call | flops 134217728 | bytes 524288 | tf_op jit(solution)/shard_map/project/pallas_call | solution.py:165
  2.2 23.6 %all_to_all.10.parts = f32[32,16,512]{2,1,0:T(8,128)S(1)} all-to-all(f32[32,16,512]{2,1,0:T(8,128)S(1)} %project.1), channel_id=1, replica_groups={{88,80,72,64,56,48,40,32,24,16,8,0,120,112,104,96,92,84,76,68,60,52,44,..., dimensions={0} | all-to-all | bytes 2097152 | tf_op jit(solution)/shard_map/all_to_all | solution.py:203
  25.8 0.0 copy-done
  25.8 0.0 copy-start.1
  25.8 0.0 copy-start.3
  25.8 0.0 copy-start.4
  25.8 0.5 forward.1
  26.3 0.0 collective-permute-start
  26.9 0.7 %collective-permute-done.other = f32[16,2048]{1,0:T(8,128)S(1)} collective-permute-done((f32[16,2048]{1,0:T(8,128)S(1)}, f32[16,2048]{1,0:T(8,128)S(1)}, u32[]{:S(2)}, u32[]{:S(2)}) %collective-permute-start) | collective-permute-done | bytes 131104 | tf_op jit(solution)/shard_map/ppermute | solution.py:206
  27.6 0.6 %middle.1 = (f32[16,2048]{1,0:T(8,128)S(1)}, bf16[2048,512]{1,0:T(8,128)(2,1)S(1)}) custom-call(f32[16,2048]{1,0:T(8,128)S(1)} %get-tuple-element.8.mine, f32[16,2048]{1,0:T(8,128)S(1)} %collective-permute-done.other, bf16[512,2048]{1,0:T(8,128)(2,1)S(1)} %copy-done), custom_call_target="tpu_custom_call" | custom-call | flops 1048576 | bytes 2359296 | tf_op jit(solution)/shard_map/middle/pallas_call | solution.py:165
  28.2 2.2 %collective-permute-start.1 = (f32[16,2048]{1,0:T(8,128)S(1)}, f32[16,2048]{1,0:T(8,128)S(1)}, u32[]{:S(2)}, u32[]{:S(2)}) collective-permute-start(f32[16,2048]{1,0:T(8,128)S(1)} %get-tuple-element.9.mine), channel_id=1, source_target_pairs={{0,6},{1,7},{2,4},{3,5},{4,2},{5,3},{6,0},{7,1},{8,14},{9,15},{10,... | collective-permute-start | bytes 393224 | tf_op jit(solution)/shard_map/ppermute | solution.py:209
  30.5 0.0 copy-done.1
  30.5 0.0 copy-done.3
  30.5 0.0 copy-done.4
  30.5 4.1 %lever.1 = (f32[256,512]{1,0:T(8,128)S(1)}, f32[16,2048]{1,0:T(8,128)S(1)}) custom-call(f32[1,512]{1,0:T(1,128)S(1)} %bitcast.4, f32[1,2048]{1,0:T(1,128)S(1)} %bitcast.2, f32[1]{0:T(128)S(6)} %copy.8.ridge, bf16[256,512]{1,0:T(8,128)(2,1)S(1)} %copy-done.1, bf16[2048,512]{1,0:T(8,128)(2,1)S(1)} %get-tuple-element.10.turned_0, ...), custom_call_target="tpu_custom_call" | custom-call | flops 1610612736 | bytes 4466692 | tf_op jit(solution)/shard_map/lever/pallas_call | solution.py:165
  34.6 0.0 collective-permute-done.1.other
  34.6 0.6 %backward.1 = f32[32,16,512]{2,1,0:T(8,128)S(1)} custom-call(f32[16,2048]{1,0:T(8,128)S(1)} %get-tuple-element.9.mine, f32[16,2048]{1,0:T(8,128)S(1)} %collective-permute-done.1.other, f32[16,2048]{1,0:T(8,128)S(1)} %get-tuple-element.12.weights, bf16[2048,512]{1,0:T(8,128)(2,1)S(1)} %get-tuple-element.10.turned_0, ...), custom_call_target="tpu_custom_call" | custom-call | flops 67108864 | bytes 4587520 | tf_op jit(solution)/shard_map/backward/pallas_call | solution.py:165
  35.2 0.0 copy-start.2
  35.2 19.0 %all_to_all.11.parts = f32[32,16,512]{2,1,0:T(8,128)S(1)} all-to-all(f32[32,16,512]{2,1,0:T(8,128)S(1)} %backward.1), channel_id=1, replica_groups={{88,80,72,64,56,48,40,32,24,16,8,0,120,112,104,96,92,84,76,68,60,52,44,..., dimensions={0} | all-to-all | bytes 2097152 | tf_op jit(solution)/shard_map/all_to_all | solution.py:215
  54.2 0.0 copy-done.2
  54.2 1.3 %fit.1 = (bf16[256,512]{1,0:T(8,128)(2,1)}, bf16[256,512]{1,0:T(8,128)(2,1)}) custom-call(f32[32,16,512]{2,1,0:T(8,128)S(1)} %all_to_all.11.parts, bf16[256,512]{1,0:T(8,128)(2,1)S(1)} %copy-done.2, f32[256,512]{1,0:T(8,128)S(1)} %get-tuple-element.13.total, f32[1,512]{1,0:T(1,128)S(1)} %bitcast.5, f32[1,2048]{1,0:T(1,128)S(1)} %bitcast.3, f32[1]{0:T(128)S(6)} %copy.8.ridge, ...), custom_call_target="tpu_custom_call" | custom-call | flops 268435456 | bytes 4204548 | tf_op jit(solution)/shard_map/fit/pallas_call | solution.py:165
Async XLA Ops:
  0.6 25.2 %copy-start = (bf16[512,2048]{1,0:T(8,128)(2,1)S(1)}, bf16[512,2048]{1,0:T(8,128)(2,1)}, u32[]{:S(2)}) copy-start(bf16[512,2048]{1,0:T(8,128)(2,1)} %target_basis.3) | copy-start | bytes 6291460
  25.8 4.7 %copy-start.1 = (bf16[256,512]{1,0:T(8,128)(2,1)S(1)}, bf16[256,512]{1,0:T(8,128)(2,1)}, u32[]{:S(2)}) copy-start(bf16[256,512]{1,0:T(8,128)(2,1)} %drug_basis.5) | copy-start | bytes 786436
  25.8 4.7 %copy-start.3 = (f32[2048]{0:T(1024)S(1)}, f32[2048]{0:T(1024)}, u32[]{:S(2)}) copy-start(f32[2048]{0:T(1024)} %param.10) | copy-start | bytes 24580
  25.8 4.7 %copy-start.4 = (f32[512]{0:T(512)S(1)}, f32[512]{0:T(512)}, u32[]{:S(2)}) copy-start(f32[512]{0:T(512)} %param.9) | copy-start | bytes 6148
  26.3 1.4 %collective-permute-start = (f32[16,2048]{1,0:T(8,128)S(1)}, f32[16,2048]{1,0:T(8,128)S(1)}, u32[]{:S(2)}, u32[]{:S(2)}) collective-permute-start(f32[16,2048]{1,0:T(8,128)S(1)} %get-tuple-element.8.mine), channel_id=1, source_target_pairs={{0,1},{1,0},{2,3},{3,2},{4,5},{5,4},{6,7},{7,6},{8,9},{9,8},{10,11... | collective-permute-start | bytes 393224 | tf_op jit(solution)/shard_map/ppermute | solution.py:206
  28.2 6.4 %collective-permute-start.1 = (f32[16,2048]{1,0:T(8,128)S(1)}, f32[16,2048]{1,0:T(8,128)S(1)}, u32[]{:S(2)}, u32[]{:S(2)}) collective-permute-start(f32[16,2048]{1,0:T(8,128)S(1)} %get-tuple-element.9.mine), channel_id=1, source_target_pairs={{0,6},{1,7},{2,4},{3,5},{4,2},{5,3},{6,0},{7,1},{8,14},{9,15},{10,... | collective-permute-start | bytes 393224 | tf_op jit(solution)/shard_map/ppermute | solution.py:209
  35.2 19.0 %copy-start.2 = (bf16[256,512]{1,0:T(8,128)(2,1)S(1)}, bf16[256,512]{1,0:T(8,128)(2,1)}, u32[]{:S(2)}) copy-start(bf16[256,512]{1,0:T(8,128)(2,1)} %activity.3) | copy-start | bytes 786436

commit v11 on v10

--- a/solution.py
+++ b/solution.py
@@ -8,7 +8,7 @@
 MIB = 1024 * 1024
 PLANE, Z = 16, 4
 AHEAD = (2, 3)
-PIECES, LATE = 4, 2
+PIECES, LATE = 8, 3
 
 
 def halves(x):

time: 55.7 us -> 55.8 us (level)
  no operation moved by 1% of the time
where the time goes in v11:
time: 55.8 us; the launch traced here: 55.5 us
  blocking collectives  42.6 us (76%)
  Pallas kernels  8.59 us (15%)
  starting transfers between devices  2.23 us (4%)
  between operations  1.37 us (2%)
  waiting for transfers between devices  0.7 us (1%)
    all_to_all x1, blocking collectives, shards(): parts = lax.all_to_all(sums, ('cmp', 'tgt'), 0, 0, axis_index_groups=groups)  23.6 us
    all_to_all x1, blocking collectives, shards(): back = lax.all_to_all(back, ('cmp', 'tgt'), 0, 0, axis_index_groups=groups)  19 us
    pallas_call x6, Pallas kernels, run(): pl.pallas_call(body, out_shape=outs, in_specs=[pl.BlockSpec(memory_space=...  8.59 us
    ppermute x1, starting transfers between devices, shards(): lax.ppermute(coeff, ('cmp', 'tgt'), [(i, i ^ across) for i in devices])  2.23 us
  transfers between devices with their start and end apart: 2, of which 1 were waited for; matrix products, arithmetic and copies ran while one was open for 0% of the time, Pallas kernels for 7%

profile of v11, /device:TPU:0, one launch (start us, length us, event | category | flops | bytes accessed | tf_op | source)
XLA Modules:
  0.0 55.5 jit_solution(10046453957000927316)
XLA Ops:
  0.6 0.0 copy-start
  0.6 1.5 %project.1 = f32[32,16,512]{2,1,0:T(8,128)S(1)} custom-call(bf16[256,512]{1,0:T(8,128)(2,1)} %drug_basis.5, bf16[256,512]{1,0:T(8,128)(2,1)} %activity.3), custom_call_target="tpu_custom_call" | custom-call | flops 134217728 | bytes 524288 | tf_op jit(solution)/shard_map/project/pallas_call | solution.py:165
  2.2 23.6 %all_to_all.10.parts = f32[32,16,512]{2,1,0:T(8,128)S(1)} all-to-all(f32[32,16,512]{2,1,0:T(8,128)S(1)} %project.1), channel_id=1, replica_groups={{88,80,72,64,56,48,40,32,24,16,8,0,120,112,104,96,92,84,76,68,60,52,44,..., dimensions={0} | all-to-all | bytes 2097152 | tf_op jit(solution)/shard_map/all_to_all | solution.py:203
  25.8 0.0 copy-done
  25.8 0.0 copy-start.1
  25.8 0.0 copy-start.3
  25.8 0.0 copy-start.4
  25.8 0.5 forward.1
  26.3 0.0 collective-permute-start
  26.9 0.7 %collective-permute-done.other = f32[16,2048]{1,0:T(8,128)S(1)} collective-permute-done((f32[16,2048]{1,0:T(8,128)S(1)}, f32[16,2048]{1,0:T(8,128)S(1)}, u32[]{:S(2)}, u32[]{:S(2)}) %collective-permute-start) | collective-permute-done | bytes 131104 | tf_op jit(solution)/shard_map/ppermute | solution.py:206
  27.6 0.6 %middle.1 = (f32[16,2048]{1,0:T(8,128)S(1)}, bf16[2048,512]{1,0:T(8,128)(2,1)S(1)}) custom-call(f32[16,2048]{1,0:T(8,128)S(1)} %get-tuple-element.8.mine, f32[16,2048]{1,0:T(8,128)S(1)} %collective-permute-done.other, bf16[512,2048]{1,0:T(8,128)(2,1)S(1)} %copy-done), custom_call_target="tpu_custom_call" | custom-call | flops 1048576 | bytes 2359296 | tf_op jit(solution)/shard_map/middle/pallas_call | solution.py:165
  28.2 2.2 %collective-permute-start.1 = (f32[16,2048]{1,0:T(8,128)S(1)}, f32[16,2048]{1,0:T(8,128)S(1)}, u32[]{:S(2)}, u32[]{:S(2)}) collective-permute-start(f32[16,2048]{1,0:T(8,128)S(1)} %get-tuple-element.9.mine), channel_id=1, source_target_pairs={{0,6},{1,7},{2,4},{3,5},{4,2},{5,3},{6,0},{7,1},{8,14},{9,15},{10,... | collective-permute-start | bytes 393224 | tf_op jit(solution)/shard_map/ppermute | solution.py:209
  30.5 0.0 copy-done.1
  30.5 0.0 copy-done.3
  30.5 0.0 copy-done.4
  30.5 4.1 %lever.1 = (f32[256,512]{1,0:T(8,128)S(1)}, f32[16,2048]{1,0:T(8,128)S(1)}) custom-call(f32[1,512]{1,0:T(1,128)S(1)} %bitcast.4, f32[1,2048]{1,0:T(1,128)S(1)} %bitcast.2, f32[1]{0:T(128)S(6)} %copy.8.ridge, bf16[256,512]{1,0:T(8,128)(2,1)S(1)} %copy-done.1, bf16[2048,512]{1,0:T(8,128)(2,1)S(1)} %get-tuple-element.10.turned_0, ...), custom_call_target="tpu_custom_call" | custom-call | flops 1610612736 | bytes 4466692 | tf_op jit(solution)/shard_map/lever/pallas_call | solution.py:165
  34.6 0.0 collective-permute-done.1.other
  34.6 0.6 %backward.1 = f32[32,16,512]{2,1,0:T(8,128)S(1)} custom-call(f32[16,2048]{1,0:T(8,128)S(1)} %get-tuple-element.9.mine, f32[16,2048]{1,0:T(8,128)S(1)} %collective-permute-done.1.other, f32[16,2048]{1,0:T(8,128)S(1)} %get-tuple-element.12.weights, bf16[2048,512]{1,0:T(8,128)(2,1)S(1)} %get-tuple-element.10.turned_0, ...), custom_call_target="tpu_custom_call" | custom-call | flops 67108864 | bytes 4587520 | tf_op jit(solution)/shard_map/backward/pallas_call | solution.py:165
  35.2 0.0 copy-start.2
  35.2 19.0 %all_to_all.11.parts = f32[32,16,512]{2,1,0:T(8,128)S(1)} all-to-all(f32[32,16,512]{2,1,0:T(8,128)S(1)} %backward.1), channel_id=1, replica_groups={{88,80,72,64,56,48,40,32,24,16,8,0,120,112,104,96,92,84,76,68,60,52,44,..., dimensions={0} | all-to-all | bytes 2097152 | tf_op jit(solution)/shard_map/all_to_all | solution.py:215
  54.2 0.0 copy-done.2
  54.2 1.3 %fit.1 = (bf16[256,512]{1,0:T(8,128)(2,1)}, bf16[256,512]{1,0:T(8,128)(2,1)}) custom-call(f32[32,16,512]{2,1,0:T(8,128)S(1)} %all_to_all.11.parts, bf16[256,512]{1,0:T(8,128)(2,1)S(1)} %copy-done.2, f32[256,512]{1,0:T(8,128)S(1)} %get-tuple-element.13.total, f32[1,512]{1,0:T(1,128)S(1)} %bitcast.5, f32[1,2048]{1,0:T(1,128)S(1)} %bitcast.3, f32[1]{0:T(128)S(6)} %copy.8.ridge, ...), custom_call_target="tpu_custom_call" | custom-call | flops 268435456 | bytes 4204548 | tf_op jit(solution)/shard_map/fit/pallas_call | solution.py:165
Async XLA Ops:
  0.6 25.2 %copy-start = (bf16[512,2048]{1,0:T(8,128)(2,1)S(1)}, bf16[512,2048]{1,0:T(8,128)(2,1)}, u32[]{:S(2)}) copy-start(bf16[512,2048]{1,0:T(8,128)(2,1)} %target_basis.3) | copy-start | bytes 6291460
  25.8 4.7 %copy-start.1 = (bf16[256,512]{1,0:T(8,128)(2,1)S(1)}, bf16[256,512]{1,0:T(8,128)(2,1)}, u32[]{:S(2)}) copy-start(bf16[256,512]{1,0:T(8,128)(2,1)} %drug_basis.5) | copy-start | bytes 786436
  25.8 4.7 %copy-start.3 = (f32[2048]{0:T(1024)S(1)}, f32[2048]{0:T(1024)}, u32[]{:S(2)}) copy-start(f32[2048]{0:T(1024)} %param.10) | copy-start | bytes 24580
  25.8 4.7 %copy-start.4 = (f32[512]{0:T(512)S(1)}, f32[512]{0:T(512)}, u32[]{:S(2)}) copy-start(f32[512]{0:T(512)} %param.9) | copy-start | bytes 6148
  26.3 1.4 %collective-permute-start = (f32[16,2048]{1,0:T(8,128)S(1)}, f32[16,2048]{1,0:T(8,128)S(1)}, u32[]{:S(2)}, u32[]{:S(2)}) collective-permute-start(f32[16,2048]{1,0:T(8,128)S(1)} %get-tuple-element.8.mine), channel_id=1, source_target_pairs={{0,1},{1,0},{2,3},{3,2},{4,5},{5,4},{6,7},{7,6},{8,9},{9,8},{10,11... | collective-permute-start | bytes 393224 | tf_op jit(solution)/shard_map/ppermute | solution.py:206
  28.2 6.4 %collective-permute-start.1 = (f32[16,2048]{1,0:T(8,128)S(1)}, f32[16,2048]{1,0:T(8,128)S(1)}, u32[]{:S(2)}, u32[]{:S(2)}) collective-permute-start(f32[16,2048]{1,0:T(8,128)S(1)} %get-tuple-element.9.mine), channel_id=1, source_target_pairs={{0,6},{1,7},{2,4},{3,5},{4,2},{5,3},{6,0},{7,1},{8,14},{9,15},{10,... | collective-permute-start | bytes 393224 | tf_op jit(solution)/shard_map/ppermute | solution.py:209
  35.2 19.0 %copy-start.2 = (bf16[256,512]{1,0:T(8,128)(2,1)S(1)}, bf16[256,512]{1,0:T(8,128)(2,1)}, u32[]{:S(2)}) copy-start(bf16[256,512]{1,0:T(8,128)(2,1)} %activity.3) | copy-start | bytes 786436
